TPU v7x, 256 devices: a whole 4x4x8 slice. The times are simulated.
256 devices in a mesh: lat: 8 (over y_hi, x), lon: 32 (over y_lo, z, core).
Axes of the slice: x: 4, y: 4 (y_hi: 2, y_lo: 2; y = y_hi * 2 + y_lo), z: 8, core: 2. Of those that a mesh axis runs over, the one named last changes fastest.
Arguments:
- noise: float32 [2, 16, 512, 4096], P(None, None, 'lat', 'lon'), may hold values from -6 to 6
- land_mask: int32 [16, 512, 4096], P(None, 'lat', 'lon'), may hold values from 0 to 1, as said below
- east_coef: float32 [16, 512, 4096], P(None, 'lat', 'lon'), may hold values from 0 to 0.24, as said below
- north_coef: float32 [16, 512, 4096], P(None, 'lat', 'lon'), may hold values from 0 to 0.24, as said below
Outputs:
- state_field: float32 [2, 16, 512, 4096], P(None, None, 'lat', 'lon')
Inputs may be any that keep to these rules, and one draw needn't show every extreme that they name: `land_mask`: 1 marks ocean; a cell that is ocean at a level is ocean at every shallower level; along the top row the mask at column j equals that at column 4095 - j. `east_coef`: zero on every face with land on either side (the top row's northern face joins column j to column 4095 - j). `north_coef`: zero on every face with land on either side (the top row's northern face joins column j to column 4095 - j).
All inputs are finite; a program needn't handle non-finite values.
Results may differ from a plain program's by a relative error of at most 0.00002.
Values sent between devices are 32-bit elements; how exact they have to be, the bound alone decides.
No kernel may reach another device: no remote copies, remote signals or barrier semaphores. Data moves between devices by JAX's collectives and lax.ppermute only.
A program may use at most 64 MiB of HBM per device.

v0:
```python
import jax
import jax.numpy as jnp
from jax import lax
from jax.sharding import PartitionSpec as P

ITERS = 2


def passed_along(block, axis, distance):
    devices = range(lax.axis_size(axis))
    route = [((i - distance) % len(devices), i) for i in devices]
    return lax.ppermute(block, axis, route)


def from_behind(block, axis, distance):
    devices = range(lax.axis_size(axis))
    route = [(i - distance, i) for i in devices if i - distance in devices]
    return lax.ppermute(block, axis, route)


def extended(block, sides, width, periodic):
    for axis, dim in sides:
        count = lax.axis_size(axis)
        forward = [(i, i + 1) for i in range(count - 1)]
        if periodic:
            forward.append((count - 1, 0))
        backward = [(target, source) for source, target in forward]
        low = lax.ppermute(
            lax.slice_in_dim(block, block.shape[dim] - width, None, axis=dim), axis, forward
        )
        high = lax.ppermute(lax.slice_in_dim(block, 0, width, axis=dim), axis, backward)
        block = jnp.concatenate([low, block, high], axis=dim)
    return block


def local(noise, land_mask, east_coef, north_coef):
    ocean_mask = land_mask.astype(jnp.float32)
    width = noise.shape[3]
    height = noise.shape[2]
    state_field = noise * ocean_mask
    coef_cols = lax.broadcasted_iota(jnp.int32, east_coef.shape, 2)
    coef_rows = lax.broadcasted_iota(jnp.int32, east_coef.shape, 1)
    west_edge = passed_along(east_coef[:, :, -1:], "lon", 1)
    west_coef = jnp.where(coef_cols == 0, west_edge, jnp.roll(east_coef, 1, axis=2))
    south_edge = from_behind(north_coef[:, -1:, :], "lat", 1)
    south_coef = jnp.where(coef_rows == 0, south_edge, jnp.roll(north_coef, 1, axis=1))
    state_cols = lax.broadcasted_iota(jnp.int32, state_field.shape, 3)
    state_rows = lax.broadcasted_iota(jnp.int32, state_field.shape, 2)
    is_top = lax.axis_index("lat") == lax.axis_size("lat") - 1
    for iteration in range(ITERS):
        row_edges = jnp.stack([state_field[:, :, 0, :], state_field[:, :, -1, :]], axis=2)
        row_ext = extended(row_edges, (("lat", 2),), 1, False)
        col_edges = jnp.stack([state_field[:, :, :, 0], state_field[:, :, :, -1]], axis=3)
        col_ext = extended(col_edges, (("lon", 3),), 1, True)
        top_row = state_field[:, :, -1, :]
        whole_row = lax.all_gather(top_row, "lon", axis=2, tiled=True)
        flipped = jnp.flip(whole_row, axis=2)
        fold_ghost = lax.dynamic_slice_in_dim(flipped, lax.axis_index("lon") * width, width, 2)
        upper_row = jnp.where(is_top, fold_ghost, row_ext[:, :, 3, :])
        lower_row = row_ext[:, :, 0, :]
        east_vals = jnp.where(
            state_cols == width - 1, col_ext[:, :, :, 3:4], jnp.roll(state_field, -1, axis=3)
        )
        west_vals = jnp.where(
            state_cols == 0, col_ext[:, :, :, 0:1], jnp.roll(state_field, 1, axis=3)
        )
        north_vals = jnp.where(
            state_rows == height - 1, upper_row[:, :, None, :], jnp.roll(state_field, -1, axis=2)
        )
        south_vals = jnp.where(
            state_rows == 0, lower_row[:, :, None, :], jnp.roll(state_field, 1, axis=2)
        )
        net_flux = east_coef * (east_vals - state_field) - west_coef * (state_field - west_vals)
        net_flux = (
            net_flux
            + north_coef * (north_vals - state_field)
            - south_coef * (state_field - south_vals)
        )
        state_field = ocean_mask * (state_field + net_flux)
    return state_field


def solution(mesh):
    return jax.shard_map(
        local,
        mesh=mesh,
        in_specs=(
            P(None, None, "lat", "lon"),
            P(None, "lat", "lon"),
            P(None, "lat", "lon"),
            P(None, "lat", "lon"),
        ),
        out_specs=P(None, None, "lat", "lon"),
        check_vma=False,
    )
```

profile of v0, /device:TPU:16, one launch (start us, length us, event | category | flops | bytes accessed | tf_op | source)
XLA Modules:
  0.0 200.4 jit_solution(7792330129426021371)
XLA Ops:
  1.7 2.8 %copy.84 = f32[2,16,64,128]{2,1,0,3:T(8,128)} copy(f32[2,16,64,128]{3,2,1,0:T(8,128)S(1)} %copy-done.3) | data formatting | bytes 2097152 | tf_op args[0]
  4.5 2.0 broadcast_multiply_fusion
  6.5 2.8 %fusion.30 = (f32[2,16,1,128]{2,1,0,3:T(8,128)}, f32[2,16,1,128]{2,1,0,3:T(8,128)}) fusion(f32[2,16,64,128]{2,1,0,3:T(8,128)S(1)} %broadcast_multiply_fusion), kind=kLoop, calls=%fused_computation.47 | loop fusion | bytes 65536 | tf_op jit(solution)/shard_map/slice | solution.py:55
  9.3 2.7 %copy.91 = f32[2,16,1,128]{3,1,2,0:T(8,128)S(1)} copy(f32[2,16,1,128]{2,1,0,3:T(8,128)} %get-tuple-element.14) | data formatting | bytes 32768 | tf_op jit(solution)/shard_map/slice | solution.py:51
  11.9 4.4 %collective-permute-start.3 = (f32[2,16,1,128]{3,1,2,0:T(8,128)S(1)}, f32[2,16,1,128]{3,1,2,0:T(8,128)S(1)}, u32[]{:S(2)}, u32[]{:S(2)}) collective-permute-start(f32[2,16,1,128]{3,1,2,0:T(8,128)S(1)} %copy.91), channel_id=1, source_target_pairs={{32,0},{64,32},{96,64},{128,96},{160,128},{192,160},{224,192},{33,... | collective-permute-start | bytes 49160 | tf_op jit(solution)/shard_map/ppermute | solution.py:31
  16.3 2.7 %copy.90 = f32[2,16,1,128]{3,1,2,0:T(8,128)S(1)} copy(f32[2,16,1,128]{2,1,0,3:T(8,128)} %get-tuple-element.13) | data formatting | bytes 32768 | tf_op jit(solution)/shard_map/slice | solution.py:55
  19.0 1.9 collective-permute-start.5
  20.9 2.4 %copy.85 = f32[16,64,128]{1,0,2:T(8,128)} copy(f32[16,64,128]{2,1,0:T(8,128)} %param.6) | data formatting | bytes 1048576 | tf_op args[2]
  24.1 6.6 %collective-permute-start = (f32[2,16,64,1]{2,1,0,3:T(8,128)S(1)}, f32[2,16,64,1]{2,1,0,3:T(8,128)S(1)}, u32[]{:S(2)}, u32[]{:S(2)}) collective-permute-start(f32[2,16,64,1]{2,1,0,3:T(8,128)S(1)} %get-tuple-element.18), channel_id=1, source_target_pairs={{1,0},{2,1},{3,2},{4,3},{5,4},{6,5},{7,6},{8,7},{9,8},{10,9},{11,1... | collective-permute-start | bytes 24584 | tf_op jit(solution)/shard_map/ppermute | solution.py:31
  30.7 37.0 %all-gather = f32[2,16,1,4096]{3,1,2,0:T(8,128)} all-gather(f32[2,16,1,128]{3,1,2,0:T(8,128)S(1)} %copy.90), channel_id=2, replica_groups=mesh['lat'=8,'lon'=32] {'lon'}, dimensions={3}, use_global_device_ids=true | all-gather | bytes 540672 | tf_op jit(solution)/shard_map/all_gather | solution.py:56
  67.7 2.8 %fusion.31 = (f32[2,16,63,128]{2,1,0,3:T(8,128)}, f32[2,16,63,128]{2,1,0,3:T(8,128)}) fusion(f32[2,16,64,128]{2,1,0,3:T(8,128)S(1)} %broadcast_multiply_fusion), kind=kLoop, calls=%fused_computation.48 | loop fusion | bytes 4128768 | tf_op jit(solution)/shard_map/jit(_roll_static)/slice | solution.py:71
  70.4 2.7 %fusion.33 = (f32[2,16,64,127]{2,1,0,3:T(8,128)}, f32[2,16,64,127]{2,1,0,3:T(8,128)}) fusion(f32[2,16,64,128]{2,1,0,3:T(8,128)S(1)} %broadcast_multiply_fusion), kind=kLoop, calls=%fused_computation.50 | loop fusion | bytes 4161536 | tf_op jit(solution)/shard_map/jit(_roll_static)/slice | solution.py:65
  74.4 2.4 %copy.89 = f32[16,64,128]{1,0,2:T(8,128)} copy(f32[16,64,128]{2,1,0:T(8,128)} %param.7) | data formatting | bytes 1048576 | tf_op args[3]
  76.8 10.9 %rev.7 = f32[2,16,4096]{2,1,0:T(8,128)} reverse(f32[2,16,4096]{2,1,0:T(8,128)S(1)} %bitcast.18), dimensions={2} | reverse | bytes 1048576 | tf_op jit(solution)/shard_map/jit(_flip)/rev | solution.py:57
  87.7 2.2 %collective-permute-start.4 = (f32[16,1,128]{2,1,0:T(1,128)S(1)}, f32[16,1,128]{2,1,0:T(1,128)S(1)}, u32[]{:S(2)}, u32[]{:S(2)}) collective-permute-start(f32[16,1,128]{2,1,0:T(1,128)S(1)} %slice.93), channel_id=1, source_target_pairs={{0,32},{32,64},{64,96},{96,128},{128,160},{160,192},{192,224},{1,3... | collective-permute-start | bytes 24584 | tf_op jit(solution)/shard_map/ppermute | solution.py:18
  90.2 1.4 copy.88
  91.6 5.3 %collective-permute-done.4 = f32[16,1,128]{2,1,0:T(1,128)S(1)} collective-permute-done((f32[16,1,128]{2,1,0:T(1,128)S(1)}, f32[16,1,128]{2,1,0:T(1,128)S(1)}, u32[]{:S(2)}, u32[]{:S(2)}) %collective-permute-start.4) | collective-permute-done | bytes 8224 | tf_op jit(solution)/shard_map/ppermute | solution.py:18
  97.0 1.4 copy.93
  99.4 8.6 %fusion.6 = f32[2,16,64,128]{2,1,0,3:T(8,128)S(1)} fusion(f32[2,16,64,1]{2,1,0,3:T(8,128)S(1)} %get-tuple-element.18, f32[2,16,64,127]{2,1,0,3:T(8,128)} %get-tuple-element.20, f32[2,16,64,127]{2,1,0,3:T(8,128)} %get-tuple-element.19, f32[2,16,64,1]{2,1,0,3:T(8,128)S(1)} %get-tuple-element.17, f32[2,16,1,128]{2,1,0,3:T(8,128)} %get-tuple-element.14, ...), kind=kLoop, calls=%fused_computation.7 | loop fusion | flops 5767168 | bytes 8962432 | tf_op jit(solution)/shard_map/mul | solution.py:79
  107.9 2.7 %fusion.26 = (f32[2,16,1,128]{2,1,0,3:T(8,128)}, f32[2,16,1,128]{2,1,0,3:T(8,128)}) fusion(f32[2,16,64,128]{2,1,0,3:T(8,128)S(1)} %fusion.6), kind=kLoop, calls=%fused_computation.43 | loop fusion | bytes 65536 | tf_op jit(solution)/shard_map/slice | solution.py:55
  110.6 2.7 %copy.96 = f32[2,16,1,128]{3,1,2,0:T(8,128)S(1)} copy(f32[2,16,1,128]{2,1,0,3:T(8,128)} %get-tuple-element.5) | data formatting | bytes 32768 | tf_op jit(solution)/shard_map/slice | solution.py:55
  113.3 34.5 %all-gather.1 = f32[2,16,1,4096]{3,1,2,0:T(8,128)} all-gather(f32[2,16,1,128]{3,1,2,0:T(8,128)S(1)} %copy.96), channel_id=3, replica_groups=mesh['lat'=8,'lon'=32] {'lon'}, dimensions={3}, use_global_device_ids=true | all-gather | bytes 540672 | tf_op jit(solution)/shard_map/all_gather | solution.py:56
  147.7 1.9 collective-permute-start.9
  149.7 2.7 %fusion.27 = (f32[2,16,63,128]{2,1,0,3:T(8,128)}, f32[2,16,63,128]{2,1,0,3:T(8,128)}) fusion(f32[2,16,64,128]{2,1,0,3:T(8,128)S(1)} %fusion.6), kind=kLoop, calls=%fused_computation.44 | loop fusion | bytes 4128768 | tf_op jit(solution)/shard_map/jit(_roll_static)/slice | solution.py:71
  152.4 2.7 %fusion.29 = (f32[2,16,64,127]{2,1,0,3:T(8,128)}, f32[2,16,64,127]{2,1,0,3:T(8,128)}) fusion(f32[2,16,64,128]{2,1,0,3:T(8,128)S(1)} %fusion.6), kind=kLoop, calls=%fused_computation.46 | loop fusion | bytes 4161536 | tf_op jit(solution)/shard_map/jit(_roll_static)/slice | solution.py:65
  155.1 2.7 %copy.97 = f32[2,16,1,128]{3,1,2,0:T(8,128)S(1)} copy(f32[2,16,1,128]{2,1,0,3:T(8,128)} %get-tuple-element.6) | data formatting | bytes 32768 | tf_op jit(solution)/shard_map/slice | solution.py:51
  157.8 7.5 %collective-permute-start.8 = (f32[2,16,1,128]{3,1,2,0:T(8,128)S(1)}, f32[2,16,1,128]{3,1,2,0:T(8,128)S(1)}, u32[]{:S(2)}, u32[]{:S(2)}) collective-permute-start(f32[2,16,1,128]{3,1,2,0:T(8,128)S(1)} %copy.97), channel_id=1, source_target_pairs={{32,0},{64,32},{96,64},{128,96},{160,128},{192,160},{224,192},{33,... | collective-permute-start | bytes 49160 | tf_op jit(solution)/shard_map/ppermute | solution.py:31
  165.3 15.5 %rev.8 = f32[2,16,4096]{2,1,0:T(8,128)} reverse(f32[2,16,4096]{2,1,0:T(8,128)} %bitcast.19), dimensions={2} | reverse | bytes 1048576 | tf_op jit(solution)/shard_map/jit(_flip)/rev | solution.py:57
  180.8 1.4 collective-permute-start.6
  183.6 3.8 %collective-permute-done.7 = f32[2,16,64,1]{2,1,0,3:T(8,128)S(1)} collective-permute-done((f32[2,16,64,1]{2,1,0,3:T(8,128)S(1)}, f32[2,16,64,1]{2,1,0,3:T(8,128)S(1)}, u32[]{:S(2)}, u32[]{:S(2)}) %collective-permute-start.7) | collective-permute-done | bytes 8224 | tf_op jit(solution)/shard_map/ppermute | solution.py:28
  187.5 9.3 %fusion.19 = f32[2,16,64,128]{2,1,0,3:T(8,128)} fusion(f32[2,16,64,128]{2,1,0,3:T(8,128)S(1)} %fusion.6, f32[2,16,64,1]{2,1,0,3:T(8,128)S(1)} %get-tuple-element.10, f32[2,16,64,127]{2,1,0,3:T(8,128)} %get-tuple-element.12, f32[2,16,64,127]{2,1,0,3:T(8,128)} %get-tuple-element.11, f32[2,16,64,1]{2,1,0,3:T(8,128)S(1)} %get-tuple-element.9, ...), kind=kLoop, calls=%fused_computation.24 | loop fusion | flops 5505024 | bytes 8962432 | tf_op jit(solution)/shard_map/mul | solution.py:79
  196.8 3.6 %copy.101 = f32[2,16,64,128]{3,2,1,0:T(8,128)} copy(f32[2,16,64,128]{2,1,0,3:T(8,128)} %fusion.19) | data formatting | bytes 2097152 | tf_op jit(solution)/shard_map/mul | solution.py:79
  (38 shorter events, 6.4 us)
Async XLA Ops:
  0.0 1.7 copy-start.3
  11.9 86.5 %collective-permute-start.3 = (f32[2,16,1,128]{3,1,2,0:T(8,128)S(1)}, f32[2,16,1,128]{3,1,2,0:T(8,128)S(1)}, u32[]{:S(2)}, u32[]{:S(2)}) collective-permute-start(f32[2,16,1,128]{3,1,2,0:T(8,128)S(1)} %copy.91), channel_id=1, source_target_pairs={{32,0},{64,32},{96,64},{128,96},{160,128},{192,160},{224,192},{33,... | collective-permute-start | bytes 49160 | tf_op jit(solution)/shard_map/ppermute | solution.py:31
  19.0 80.2 %collective-permute-start.5 = (f32[2,16,1,128]{3,1,2,0:T(8,128)S(1)}, f32[2,16,1,128]{3,1,2,0:T(8,128)S(1)}, u32[]{:S(2)}, u32[]{:S(2)}) collective-permute-start(f32[2,16,1,128]{3,1,2,0:T(8,128)S(1)} %copy.90), channel_id=1, source_target_pairs={{0,32},{32,64},{64,96},{96,128},{128,160},{160,192},{192,224},{1,3... | collective-permute-start | bytes 49160 | tf_op jit(solution)/shard_map/ppermute | solution.py:28
  24.0 63.7 %collective-permute-start.1 = (f32[16,64,1]{1,0,2:T(8,128)S(1)}, f32[16,64,1]{1,0,2:T(8,128)S(1)}, u32[]{:S(2)}, u32[]{:S(2)}) collective-permute-start(f32[16,64,1]{1,0,2:T(8,128)S(1)} %slice.106), channel_id=1, source_target_pairs={{31,0},{0,1},{1,2},{2,3},{3,4},{4,5},{5,6},{6,7},{7,8},{8,9},{9,10... | collective-permute-start | bytes 12296 | tf_op jit(solution)/shard_map/ppermute | solution.py:12
  24.1 75.3 %collective-permute-start = (f32[2,16,64,1]{2,1,0,3:T(8,128)S(1)}, f32[2,16,64,1]{2,1,0,3:T(8,128)S(1)}, u32[]{:S(2)}, u32[]{:S(2)}) collective-permute-start(f32[2,16,64,1]{2,1,0,3:T(8,128)S(1)} %get-tuple-element.18), channel_id=1, source_target_pairs={{1,0},{2,1},{3,2},{4,3},{5,4},{6,5},{7,6},{8,7},{9,8},{10,9},{11,1... | collective-permute-start | bytes 24584 | tf_op jit(solution)/shard_map/ppermute | solution.py:31
  30.7 68.7 %collective-permute-start.2 = (f32[2,16,64,1]{2,1,0,3:T(8,128)S(1)}, f32[2,16,64,1]{2,1,0,3:T(8,128)S(1)}, u32[]{:S(2)}, u32[]{:S(2)}) collective-permute-start(f32[2,16,64,1]{2,1,0,3:T(8,128)S(1)} %get-tuple-element.17), channel_id=1, source_target_pairs={{0,1},{1,2},{2,3},{3,4},{4,5},{5,6},{6,7},{7,8},{8,9},{9,10},{10,1... | collective-permute-start | bytes 24584 | tf_op jit(solution)/shard_map/ppermute | solution.py:28
  73.2 3.6 %copy-start.2 = (f32[2,16,1,4096]{3,1,2,0:T(8,128)S(1)}, f32[2,16,1,4096]{3,1,2,0:T(8,128)}, u32[]{:S(2)}) copy-start(f32[2,16,1,4096]{3,1,2,0:T(8,128)} %all-gather) | copy-start | bytes 1572868
  73.2 16.7 %copy-start.1 = (f32[16,64,128]{2,1,0:T(8,128)S(1)}, f32[16,64,128]{2,1,0:T(8,128)}, u32[]{:S(2)}) copy-start(f32[16,64,128]{2,1,0:T(8,128)} %param.6) | copy-start | bytes 1572868
  76.8 20.1 %copy-start = (f32[16,64,128]{2,1,0:T(8,128)S(1)}, f32[16,64,128]{2,1,0:T(8,128)}, u32[]{:S(2)}) copy-start(f32[16,64,128]{2,1,0:T(8,128)} %param.7) | copy-start | bytes 1572868
  87.7 9.1 %collective-permute-start.4 = (f32[16,1,128]{2,1,0:T(1,128)S(1)}, f32[16,1,128]{2,1,0:T(1,128)S(1)}, u32[]{:S(2)}, u32[]{:S(2)}) collective-permute-start(f32[16,1,128]{2,1,0:T(1,128)S(1)} %slice.93), channel_id=1, source_target_pairs={{0,32},{32,64},{64,96},{96,128},{128,160},{160,192},{192,224},{1,3... | collective-permute-start | bytes 24584 | tf_op jit(solution)/shard_map/ppermute | solution.py:18
  147.7 35.3 %collective-permute-start.9 = (f32[2,16,1,128]{3,1,2,0:T(8,128)S(1)}, f32[2,16,1,128]{3,1,2,0:T(8,128)S(1)}, u32[]{:S(2)}, u32[]{:S(2)}) collective-permute-start(f32[2,16,1,128]{3,1,2,0:T(8,128)S(1)} %copy.96), channel_id=1, source_target_pairs={{0,32},{32,64},{64,96},{96,128},{128,160},{160,192},{192,224},{1,3... | collective-permute-start | bytes 49160 | tf_op jit(solution)/shard_map/ppermute | solution.py:28
  157.8 24.4 %collective-permute-start.8 = (f32[2,16,1,128]{3,1,2,0:T(8,128)S(1)}, f32[2,16,1,128]{3,1,2,0:T(8,128)S(1)}, u32[]{:S(2)}, u32[]{:S(2)}) collective-permute-start(f32[2,16,1,128]{3,1,2,0:T(8,128)S(1)} %copy.97), channel_id=1, source_target_pairs={{32,0},{64,32},{96,64},{128,96},{160,128},{192,160},{224,192},{33,... | collective-permute-start | bytes 49160 | tf_op jit(solution)/shard_map/ppermute | solution.py:31
  180.8 2.8 %collective-permute-start.6 = (f32[2,16,64,1]{2,1,0,3:T(8,128)S(1)}, f32[2,16,64,1]{2,1,0,3:T(8,128)S(1)}, u32[]{:S(2)}, u32[]{:S(2)}) collective-permute-start(f32[2,16,64,1]{2,1,0,3:T(8,128)S(1)} %get-tuple-element.10), channel_id=1, source_target_pairs={{1,0},{2,1},{3,2},{4,3},{5,4},{6,5},{7,6},{8,7},{9,8},{10,9},{11,1... | collective-permute-start | bytes 24584 | tf_op jit(solution)/shard_map/ppermute | solution.py:31
  182.2 5.3 %collective-permute-start.7 = (f32[2,16,64,1]{2,1,0,3:T(8,128)S(1)}, f32[2,16,64,1]{2,1,0,3:T(8,128)S(1)}, u32[]{:S(2)}, u32[]{:S(2)}) collective-permute-start(f32[2,16,64,1]{2,1,0,3:T(8,128)S(1)} %get-tuple-element.9), channel_id=1, source_target_pairs={{0,1},{1,2},{2,3},{3,4},{4,5},{5,6},{6,7},{7,8},{8,9},{9,10},{10,1... | collective-permute-start | bytes 24584 | tf_op jit(solution)/shard_map/ppermute | solution.py:28
where the time goes:
time: 203 us; the launch traced here: 200 us
  blocking collectives  71.4 us (35%)
  local copies, waits for them, and re-layouts  70.4 us (35%)
  starting transfers between devices  25.9 us (13%)
  other arithmetic  23 us (11%)
  waiting for transfers between devices  9.57 us (5%)
    all_gather x2, blocking collectives, local(): whole_row = lax.all_gather(top_row, 'lon', axis=2, tiled=True)  71.4 us
    rev x2, local copies, waits for them, and re-layouts, local(): flipped = jnp.flip(whole_row, axis=2)  26.4 us
    ppermute x4, starting transfers between devices, extended(): lax.ppermute(lax.slice_in_dim(block, 0, width, axis=dim), axis, backward)  19.9 us
    mul x2, other arithmetic, local(): state_field = ocean_mask * (state_field + net_flux)  17.9 us
    slice x4, local copies, waits for them, and re-layouts, local(): top_row = state_field[:, :, -1, :]  10.8 us
    unnamed x11, local copies, waits for them, and re-layouts  7.68 us
    slice x2, local copies, waits for them, and re-layouts, local(): jnp.roll(state_field, 1, axis=2)  5.5 us
    slice x2, local copies, waits for them, and re-layouts, local(): jnp.roll(state_field, 1, axis=3)  5.49 us
  transfers between devices with their start and end apart: 10, of which 3 were waited for; matrix products, arithmetic and copies ran while one was open for 27% of the time, Pallas kernels for 0%

commit v1 on v0

v1 whole, which is shorter than its diff:
```python
import jax
import jax.numpy as jnp
from jax import lax
from jax.experimental import pallas as pl
from jax.experimental.pallas import tpu as pltpu
from jax.sharding import PartitionSpec as P


LEVELS, ROWS, COLS = 16, 64, 128
PACKED = 72
F32 = jnp.float32
VMEM = pl.BlockSpec(memory_space=pltpu.VMEM)


def lanes(rows):
    return lax.broadcasted_iota(jnp.int32, (rows, COLS), 1)


def turned(x, shift):
    return pltpu.roll(x, shift % COLS if isinstance(shift, int) else shift, 1)


def edge_rows(noise_lo, noise_hi, mask_lo, mask_hi, east_lo, east_hi, north_lo, north_hi, out_b, out_a):
    lat = lax.axis_index("lat")
    top_block = lat == lax.axis_size("lat") - 1
    even = lax.rem(lat, 2) == 0
    lane = lanes(LEVELS)

    def lateral(u, east, west):
        return east * (turned(u, -1) - u) - west * (u - turned(u, 1))

    def inner_faces(east):
        return jnp.where(lane == COLS - 1, 0.0, east), jnp.where(lane == 0, 0.0, turned(east, 1))

    mask_t = mask_hi[:, 7, :].astype(F32)
    mask_t2 = mask_hi[:, 6, :].astype(F32)
    mask_b = mask_lo[:, 0, :].astype(F32)
    mask_b2 = mask_lo[:, 1, :].astype(F32)
    east_t, west_t = inner_faces(east_hi[:, 7, :])
    east_b, west_b = inner_faces(east_lo[:, 0, :])
    south_t = north_hi[:, 6, :]
    north_b = north_lo[:, 0, :]
    top, bottom = [], []
    top_p, bottom_p = [], []
    for m in range(2):
        u = noise_hi[m, :, 7, :] * mask_t
        v = noise_hi[m, :, 6, :] * mask_t2
        top.append(u)
        top_p.append(mask_t * (u + lateral(u, east_t, west_t) - south_t * (u - v)))
        u = noise_lo[m, :, 0, :] * mask_b
        v = noise_lo[m, :, 1, :] * mask_b2
        bottom.append(u)
        bottom_p.append(mask_b * (u + lateral(u, east_b, west_b) + north_b * (v - u)))
    top += top_p + [north_hi[:, 7, :] * mask_t, east_hi[:, 7, :] * mask_t]
    bottom += bottom_p + [mask_b, east_lo[:, 0, :] * mask_b]
    flip = jnp.where(top_block, COLS - 1 - lane, lane)
    for q in range(6):
        rows = pl.ds(q * LEVELS, LEVELS)
        out_b[rows, :] = jnp.where(even, top[q], bottom[q])
        crossed = jnp.take_along_axis(top[q], flip, axis=1)
        out_a[rows, :] = jnp.where(even, bottom[q], crossed)


def first_step(noise, mask, east, north, out_u, out_pairs, out_faces):
    lane = lanes(ROWS)
    row = lax.broadcasted_iota(jnp.int32, (ROWS, COLS), 0)
    pair = lane // 2

    def level(l, carry):
        pairs, faces = carry
        k = mask[l].astype(F32)
        e_all = east[l]
        n_all = north[l]
        e = jnp.where(lane == COLS - 1, 0.0, e_all)
        w = jnp.where(lane == 0, 0.0, turned(e_all, 1))
        n = jnp.where(row == ROWS - 1, 0.0, n_all)
        s = jnp.where(row == 0, 0.0, pltpu.roll(n_all, 1, 0))
        edge = jnp.where(lane == COLS - 1, e_all * k, k)
        faces = jnp.where(pair == l, turned(edge, 2 * l + 1), faces)
        for m in range(2):
            u = noise[m, l] * k
            flux = e * (turned(u, -1) - u) - w * (u - turned(u, 1))
            flux = flux + n * (pltpu.roll(u, ROWS - 1, 0) - u) - s * (u - pltpu.roll(u, 1, 0))
            v = k * (u + flux)
            out_u[m, l] = v
            pairs = jnp.where(pair == m * 16 + l, turned(u, m * 32 + 2 * l + 1), pairs)
            pairs = jnp.where(pair == 32 + m * 16 + l, turned(v, 64 + m * 32 + 2 * l + 1), pairs)
        return pairs, faces

    zero = jnp.zeros((ROWS, COLS), F32)
    pairs, faces = lax.fori_loop(0, LEVELS, level, (zero, zero))
    out_pairs[...] = pairs
    out_faces[...] = faces


def join_rows(
    own_b, own_a, got_b, got_a, pairs, faces, send_1, send_2, out_pairs, out_faces, out_rows, south, north, side
):
    lat = lax.axis_index("lat")
    top_block = lat == lax.axis_size("lat") - 1
    even = lax.rem(lat, 2) == 0
    even_lon = lax.rem(lax.axis_index("lon"), 2) == 0

    def part(q):
        rows = pl.ds(q * LEVELS, LEVELS)
        ob, oa, gb, ga = own_b[rows, :], own_a[rows, :], got_b[rows, :], got_a[rows, :]
        return ob, oa, jnp.where(even, gb, ga), jnp.where(even, ga, gb)

    flip = COLS - 1 - lanes(LEVELS)

    def own(q):
        ob, oa, _, _ = part(q)
        back = jnp.where(top_block, jnp.take_along_axis(oa, flip, axis=1), oa)
        return jnp.where(even, ob, back), jnp.where(even, oa, ob)

    def put(ref, q, x):
        ref[pl.ds(q * 32, LEVELS, stride=2), :] = x
        ref[pl.ds(q * 32 + 1, LEVELS, stride=2), :] = x

    own_n, own_k = own(4)
    _, _, far_n, far_s = part(4)
    ghost_n = jnp.where(top_block, far_n, own_n * far_n)
    for m in range(2):
        own_t, own_bot = own(m)
        _, _, up, down = part(m)
        _, _, up_p, down_p = part(2 + m)
        gain_s = own_k * far_s * (down - own_bot)
        gain_n = own_n * (up - own_t)
        out_rows[pl.ds(m * LEVELS, LEVELS), :] = gain_s
        out_rows[pl.ds((2 + m) * LEVELS, LEVELS), :] = gain_n
        out_rows[pl.ds((4 + m) * LEVELS, LEVELS), :] = down_p - far_s * (down - own_bot)
        out_rows[pl.ds((6 + m) * LEVELS, LEVELS), :] = up_p - ghost_n * (up - own_t)
        put(south, m, down)
        put(south, 2 + m, gain_s)
        put(north, m, up)
        put(north, 2 + m, gain_n)
    out_rows[pl.ds(8 * LEVELS, LEVELS), :] = far_s
    _, _, up_e, down_e = part(5)
    put(side, 0, down_e)
    put(side, 1, up_e)
    put(side, 2, up_e)
    put(side, 3, up_e)

    lane1 = lanes(1)
    odd1 = lax.rem(lane1, 2) == 1
    turned_s = jnp.transpose(south[...])
    turned_n = jnp.transpose(north[...])
    turned_e = jnp.transpose(side[...])
    row_s = jnp.where(odd1, turned_s[0:1, :], turned_s[COLS - 1 : COLS, :])
    row_n = jnp.where(odd1, turned_n[0:1, :], turned_n[COLS - 1 : COLS, :])
    gain = lane1 >= 64
    out_pairs[0:ROWS, :] = pairs[...]
    out_pairs[0:1, :] = pairs[0:1, :] + jnp.where(gain, row_s, 0.0)
    out_pairs[ROWS - 1 : ROWS, :] = pairs[ROWS - 1 : ROWS, :] + jnp.where(gain, row_n, 0.0)
    out_pairs[ROWS:PACKED, :] = jnp.zeros((PACKED - ROWS, COLS), F32)
    out_pairs[ROWS : ROWS + 1, :] = row_s
    out_pairs[ROWS + 1 : ROWS + 2, :] = row_n
    face_s = jnp.where(odd1, 1.0, turned_e[COLS - 1 : COLS, :])
    near = turned(turned_e[COLS - 1 : COLS, :], -32)
    mirrored = turned(turned_e[0:1, :], -32)
    face_n = jnp.where(
        top_block, jnp.where(odd1, mirrored, 1.0), jnp.where(odd1, 1.0, near)
    )
    out_faces[0:ROWS, :] = faces[...]
    out_faces[ROWS:PACKED, :] = jnp.zeros((PACKED - ROWS, COLS), F32)
    out_faces[ROWS : ROWS + 1, :] = face_s
    out_faces[ROWS + 1 : ROWS + 2, :] = face_n
    all_pairs = out_pairs[...]
    all_faces = out_faces[...]
    odd = lax.rem(lanes(PACKED), 2) == 1
    eastward = jnp.where(odd, turned(all_pairs, 1), all_faces)
    westward = jnp.where(odd, all_faces, turned(all_pairs, -1))
    send_1[...] = jnp.where(even_lon, eastward, westward)
    send_2[...] = jnp.where(even_lon, westward, eastward)


def second_step(
    u1, mask, east, north, got_1, got_2, pairs, faces, rows, out, edge_u, edge_g, edge_c, held, sem
):
    even_lon = lax.rem(lax.axis_index("lon"), 2) == 0
    lane72 = lanes(PACKED)
    row72 = lax.broadcasted_iota(jnp.int32, (PACKED, COLS), 0)
    odd = lax.rem(lane72, 2) == 1
    from_east = jnp.where(even_lon, got_1[...], got_2[...])
    from_west = jnp.where(even_lon, got_2[...], got_1[...])
    ghost = jnp.where(odd, from_west, from_east)
    mine = pairs[...]
    face = faces[...] * jnp.where(odd, turned(from_west, 1), turned(from_east, -1))
    face = jnp.where(lane72 < 32, face, turned(face, 32))
    gain = turned(face * (ghost - mine), 64)
    edge_u[...] = mine + gain
    edge_g[...] = jnp.where(row72 < ROWS, ghost - gain, gain)
    edge_c[...] = face

    lane = lanes(ROWS)
    lane1 = lanes(1)
    row = lax.broadcasted_iota(jnp.int32, (ROWS, COLS), 0)
    first, last = lane == 0, lane == COLS - 1
    side = first | last
    side1 = (lane1 == 0) | (lane1 == COLS - 1)

    def copy(m, l):
        return pltpu.make_async_copy(held.at[m, l], out.at[m, l], sem.at[m, l])

    def line(q, l):
        return rows[pl.ds(q * LEVELS + l, 1), :]

    def level(l, carry):
        k = mask[l].astype(F32)
        e = east[l]
        n = north[l]
        w = jnp.where(first, turned(edge_c[0:ROWS, :], COLS - 1 - 2 * l), turned(e, 1))
        s = jnp.where(row == 0, line(8, l), pltpu.roll(n, 1, 0))
        for m in range(2):
            shift = 63 - m * 32 - 2 * l
            u = u1[m, l]
            u = jnp.where(row == 0, u + line(m, l), u)
            u = jnp.where(row == ROWS - 1, u + line(2 + m, l), u)
            ghosts = turned(edge_g[...], shift)
            u = jnp.where(side, turned(edge_u[0:ROWS, :], shift), u)
            below = line(4 + m, l) + jnp.where(side1, ghosts[ROWS : ROWS + 1, :], 0.0)
            above = line(6 + m, l) + jnp.where(side1, ghosts[ROWS + 1 : ROWS + 2, :], 0.0)
            u_e = jnp.where(last, ghosts[0:ROWS, :], turned(u, -1))
            u_w = jnp.where(first, ghosts[0:ROWS, :], turned(u, 1))
            u_n = jnp.where(row == ROWS - 1, above, pltpu.roll(u, ROWS - 1, 0))
            u_s = jnp.where(row == 0, below, pltpu.roll(u, 1, 0))
            flux = e * (u_e - u) - w * (u - u_w)
            flux = flux + n * (u_n - u) - s * (u - u_s)
            held[m, l] = k * (u + flux)
            copy(m, l).start()
        return carry

    lax.fori_loop(0, LEVELS, level, 0)

    def finish(l, carry):
        for m in range(2):
            copy(m, l).wait()
        return carry

    lax.fori_loop(0, LEVELS, finish, 0)


def block(shape, row):
    lead = len(shape) - 2
    return pl.BlockSpec(shape, lambda i: (0,) * lead + (row, 0))


def struct(*shape):
    return jax.ShapeDtypeStruct(shape, F32)


def cost(us):
    return pl.CostEstimate(flops=int(us * 4e6), bytes_accessed=int(us * 3e6), transcendentals=0)


PARAMS = pltpu.CompilerParams(vmem_limit_bytes=32 * 1024 * 1024)


def local(noise, land_mask, east_coef, north_coef):
    n_lat, n_lon = lax.axis_size("lat"), lax.axis_size("lon")
    member_rows = [block((2, LEVELS, 8, COLS), 0), block((2, LEVELS, 8, COLS), ROWS // 8 - 1)]
    level_rows = [block((LEVELS, 8, COLS), 0), block((LEVELS, 8, COLS), ROWS // 8 - 1)]
    message = struct(6 * LEVELS, COLS)
    send_b, send_a = pl.pallas_call(
        edge_rows,
        grid=(1,),
        in_specs=member_rows + level_rows * 3,
        out_specs=[pl.BlockSpec((6 * LEVELS, COLS), lambda i: (0, 0))] * 2,
        out_shape=[message] * 2,
        compiler_params=PARAMS,
        cost_estimate=cost(1),
        name="edge_rows",
    )(noise, noise, land_mask, land_mask, east_coef, east_coef, north_coef, north_coef)

    route_b = [(i, i ^ 1) for i in range(n_lat)]
    route_a = []
    for k in range(n_lon):
        for i in range(1, n_lat - 1):
            route_a.append((i * n_lon + k, (((i - 1) ^ 1) + 1) * n_lon + k))
        route_a.append(((n_lat - 1) * n_lon + k, n_lat * n_lon - 1 - k))
    got_b = lax.ppermute(send_b, "lat", route_b)
    got_a = lax.ppermute(send_a, ("lat", "lon"), route_a)

    u1, pairs, faces = pl.pallas_call(
        first_step,
        in_specs=[VMEM] * 4,
        out_specs=[VMEM] * 3,
        out_shape=[struct(2, LEVELS, ROWS, COLS), struct(ROWS, COLS), struct(ROWS, COLS)],
        compiler_params=PARAMS,
        cost_estimate=cost(2),
        name="first_step",
    )(noise, land_mask, east_coef, north_coef)

    packed = struct(PACKED, COLS)
    send_1, send_2, pairs, faces, rows = pl.pallas_call(
        join_rows,
        in_specs=[VMEM] * 6,
        out_specs=[VMEM] * 5,
        out_shape=[packed] * 4 + [struct(9 * LEVELS, COLS)],
        scratch_shapes=[pltpu.VMEM((COLS, COLS), F32)] * 3,
        compiler_params=PARAMS,
        cost_estimate=cost(1),
        name="join_rows",
    )(send_b, send_a, got_b, got_a, pairs, faces)

    route_1 = [(k, k ^ 1) for k in range(n_lon)]
    route_2 = [(k, (((k + n_lon - 1) % n_lon ^ 1) + 1) % n_lon) for k in range(n_lon)]
    got_1 = lax.ppermute(send_1, "lon", route_1)
    got_2 = lax.ppermute(send_2, "lon", route_2)

    return pl.pallas_call(
        second_step,
        in_specs=[VMEM] * 9,
        out_specs=pl.BlockSpec(memory_space=pl.ANY),
        out_shape=struct(2, LEVELS, ROWS, COLS),
        scratch_shapes=[pltpu.VMEM((PACKED, COLS), F32)] * 3
        + [pltpu.VMEM((2, LEVELS, ROWS, COLS), F32), pltpu.SemaphoreType.DMA((2, LEVELS))],
        compiler_params=PARAMS,
        cost_estimate=cost(2),
        name="second_step",
    )(u1, land_mask, east_coef, north_coef, got_1, got_2, pairs, faces, rows)


def solution(mesh):
    return jax.shard_map(
        local,
        mesh=mesh,
        in_specs=(
            P(None, None, "lat", "lon"),
            P(None, "lat", "lon"),
            P(None, "lat", "lon"),
            P(None, "lat", "lon"),
        ),
        out_specs=P(None, None, "lat", "lon"),
        check_vma=False,
    )
```

time: 203 us -> 29 us (0.14); the launches traced: 200 us -> 28.7 us
  blocking collectives: 71.4 us -> 0 us
  local copies, waits for them, and re-layouts: 70.4 us -> 4.37 us
  other arithmetic: 23 us -> 0 us
  starting transfers between devices: 25.9 us -> 12.1 us
  Pallas kernels: 0 us -> 7.76 us
  waiting for transfers between devices: 9.57 us -> 4.42 us
    all_gather x2 -> x0, blocking collectives: 71.4 us -> none  [local(): whole_row = lax.all_gather(top_row, 'lon', axis=2, tiled=True)]
    slice x15 -> x0, local copies, waits for them, and re-layouts: 28.9 us -> none  [the longest x4 10.8 us: local(): top_row = state_field[:, :, -1, :]]
    rev x2 -> x0, local copies, waits for them, and re-layouts: 26.4 us -> none  [local(): flipped = jnp.flip(whole_row, axis=2)]
    mul x3 -> x0, other arithmetic: 19.9 us -> none  [the longest x2 17.9 us: local(): state_field = ocean_mask * (state_field + net_flux)]
    ppermute x10 -> x4, starting transfers between devices: 25.9 us -> 12.1 us  [the longest x1 6.71 us: local(): got_2 = lax.ppermute(send_2, 'lon', route_2)]
    pallas_call x0 -> x4, Pallas kernels: none -> 7.76 us  [the longest x1 4.19 us: local(): pl.pallas_call(second_step, in_specs=[VMEM] * 9, out_specs=pl.BlockSpec(m...]
    ppermute x10 -> x4, waiting for transfers between devices: 9.57 us -> 4.42 us  [the longest x1 2.78 us: local(): got_a = lax.ppermute(send_a, ('lat', 'lon'), route_a)]
    mul x1 -> x0, local copies, waits for them, and re-layouts: 3.63 us -> none  [local(): state_field = ocean_mask * (state_field + net_flux)]
  transfers between devices with their start and end apart: 10 -> 4, of which waited for: 3 -> 2; matrix products, arithmetic and copies ran while one was open for 27% -> 0% of each run, Pallas kernels for 0% -> 10%
where the time goes in v1:
time: 29 us; the launch traced here: 28.7 us
  starting transfers between devices  12.1 us (42%)
  Pallas kernels  7.76 us (27%)
  waiting for transfers between devices  4.42 us (15%)
  local copies, waits for them, and re-layouts  4.37 us (15%)
    ppermute x1, starting transfers between devices, local(): got_2 = lax.ppermute(send_2, 'lon', route_2)  6.71 us
    unnamed x14, local copies, waits for them, and re-layouts  4.37 us
    pallas_call x1, Pallas kernels, local(): pl.pallas_call(second_step, in_specs=[VMEM] * 9, out_specs=pl.BlockSpec(m...  4.19 us
    ppermute x1, starting transfers between devices, local(): got_a = lax.ppermute(send_a, ('lat', 'lon'), route_a)  3.76 us
    pallas_call x1, Pallas kernels, local(): pl.pallas_call(first_step, in_specs=[VMEM] * 4, out_specs=[VMEM] * 3, out...  2.99 us
    ppermute x1, waiting for transfers between devices, local(): got_a = lax.ppermute(send_a, ('lat', 'lon'), route_a)  2.78 us
    ppermute x1, waiting for transfers between devices, local(): got_2 = lax.ppermute(send_2, 'lon', route_2)  1.64 us
    ppermute x1, starting transfers between devices, local(): got_b = lax.ppermute(send_b, 'lat', route_b)  1.56 us
  transfers between devices with their start and end apart: 4, of which 2 were waited for; matrix products, arithmetic and copies ran while one was open for 0% of the time, Pallas kernels for 10%

profile of v1, /device:TPU:16, one launch (start us, length us, event | category | flops | bytes accessed | tf_op | source)
XLA Modules:
  0.0 28.7 jit_solution(2717166379126695625)
XLA Ops:
  0.0 0.0 copy-start
  0.0 1.2 %copy-done = f32[2,16,64,128]{3,2,1,0:T(8,128)S(1)} copy-done((f32[2,16,64,128]{3,2,1,0:T(8,128)S(1)}, f32[2,16,64,128]{3,2,1,0:T(8,128)}, u32[]{:S(2)}) %copy-start) | copy-done | bytes 1048600
  1.2 0.0 copy-start.1
  1.2 1.0 %copy-done.1 = s32[16,64,128]{2,1,0:T(8,128)S(1)} copy-done((s32[16,64,128]{2,1,0:T(8,128)S(1)}, s32[16,64,128]{2,1,0:T(8,128)}, u32[]{:S(2)}) %copy-start.1) | copy-done | bytes 524312
  2.3 0.0 copy-start.3
  2.3 1.0 %copy-done.3 = f32[16,64,128]{2,1,0:T(8,128)S(1)} copy-done((f32[16,64,128]{2,1,0:T(8,128)S(1)}, f32[16,64,128]{2,1,0:T(8,128)}, u32[]{:S(2)}) %copy-start.3) | copy-done | bytes 524312
  3.3 0.0 copy-start.5
  3.3 1.0 %copy-done.5 = f32[16,64,128]{2,1,0:T(8,128)S(1)} copy-done((f32[16,64,128]{2,1,0:T(8,128)S(1)}, f32[16,64,128]{2,1,0:T(8,128)}, u32[]{:S(2)}) %copy-start.5) | copy-done | bytes 524312
  4.4 0.3 edge_rows.1
  4.6 1.6 %collective-permute-start = (f32[96,128]{1,0:T(8,128)S(1)}, f32[96,128]{1,0:T(8,128)S(1)}, u32[]{:S(2)}, u32[]{:S(2)}) collective-permute-start(f32[96,128]{1,0:T(8,128)S(1)} %get-tuple-element.16.own_b), channel_id=1, source_target_pairs={{0,32},{32,0},{64,96},{96,64},{128,160},{160,128},{192,224},{224,1... | collective-permute-start | bytes 147464 | tf_op jit(solution)/shard_map/ppermute | solution.py:281
  6.2 3.8 %collective-permute-start.1 = (f32[96,128]{1,0:T(8,128)S(1)}, f32[96,128]{1,0:T(8,128)S(1)}, u32[]{:S(2)}, u32[]{:S(2)}) collective-permute-start(f32[96,128]{1,0:T(8,128)S(1)} %get-tuple-element.17.own_a), channel_id=1, source_target_pairs={{32,64},{64,32},{96,128},{128,96},{160,192},{192,160},{224,255},{3... | collective-permute-start | bytes 147464 | tf_op jit(solution)/shard_map/ppermute | solution.py:282
  9.9 0.0 copy-start.2
  10.0 0.0 copy-start.4
  10.0 0.0 copy-start.6
  10.0 3.0 %first_step.1 = (f32[2,16,64,128]{3,2,1,0:T(8,128)S(1)}, f32[64,128]{1,0:T(8,128)S(1)}, f32[64,128]{1,0:T(8,128)S(1)}) custom-call(f32[2,16,64,128]{3,2,1,0:T(8,128)S(1)} %copy-done, s32[16,64,128]{2,1,0:T(8,128)S(1)} %copy-done.1, f32[16,64,128]{2,1,0:T(8,128)S(1)} %copy-done.3, f32[16,64,128]{2,1,0:T(8,128)S(1)} %copy-done.5), custom_call_target="tpu_custom_call" | custom-call | flops 8000000 | bytes 6000000 | tf_op jit(solution)/shard_map/first_step/pallas_call | solution.py:284
  13.0 0.0 collective-permute-done.got_b
  13.0 2.8 %collective-permute-done.1.got_a = f32[96,128]{1,0:T(8,128)S(1)} collective-permute-done((f32[96,128]{1,0:T(8,128)S(1)}, f32[96,128]{1,0:T(8,128)S(1)}, u32[]{:S(2)}, u32[]{:S(2)}) %collective-permute-start.1) | collective-permute-done | bytes 49184 | tf_op jit(solution)/shard_map/ppermute | solution.py:282
  15.8 0.3 %join_rows.1 = (f32[72,128]{1,0:T(8,128)S(1)}, f32[72,128]{1,0:T(8,128)S(1)}, f32[72,128]{1,0:T(8,128)S(1)}, f32[72,128]{1,0:T(8,128)S(1)}, f32[144,128]{1,0:T(8,128)S(1)}) custom-call(f32[96,128]{1,0:T(8,128)S(1)} %get-tuple-element.16.own_b, f32[96,128]{1,0:T(8,128)S(1)} %get-tuple-element.17.own_a, f32[96,128]{1,0:T(8,128)S(1)} %collective-permute-done.got_b, ...), custom_call_target="tpu_custom_call" | custom-call | flops 4000000 | bytes 3000000 | tf_op jit(solution)/shard_map/join_rows/pallas_call | solution.py:295
  16.1 0.1 collective-permute-start.2
  16.2 6.7 %collective-permute-start.3 = (f32[72,128]{1,0:T(8,128)S(1)}, f32[72,128]{1,0:T(8,128)S(1)}, u32[]{:S(2)}, u32[]{:S(2)}) collective-permute-start(f32[72,128]{1,0:T(8,128)S(1)} %get-tuple-element.21), channel_id=1, source_target_pairs={{0,31},{1,2},{2,1},{3,4},{4,3},{5,6},{6,5},{7,8},{8,7},{9,10},{10,... | collective-permute-start | bytes 110600 | tf_op jit(solution)/shard_map/ppermute | solution.py:309
  22.9 0.0 collective-permute-done.2.got_1
  22.9 1.6 %collective-permute-done.3.got_2 = f32[72,128]{1,0:T(8,128)S(1)} collective-permute-done((f32[72,128]{1,0:T(8,128)S(1)}, f32[72,128]{1,0:T(8,128)S(1)}, u32[]{:S(2)}, u32[]{:S(2)}) %collective-permute-start.3) | collective-permute-done | bytes 36896 | tf_op jit(solution)/shard_map/ppermute | solution.py:309
  24.5 0.0 copy-done.2
  24.5 0.0 copy-done.4
  24.5 0.0 copy-done.6
  24.5 4.2 %second_step.1 = f32[2,16,64,128]{3,2,1,0:T(8,128)} custom-call(f32[2,16,64,128]{3,2,1,0:T(8,128)S(1)} %get-tuple-element.15.u1, s32[16,64,128]{2,1,0:T(8,128)S(1)} %copy-done.2, f32[16,64,128]{2,1,0:T(8,128)S(1)} %copy-done.4, f32[16,64,128]{2,1,0:T(8,128)S(1)} %copy-done.6, f32[72,128]{1,0:T(8,128)S(1)} %collective-permute-done.2.got_1, ...), custom_call_target="tpu_custom_call" | custom-call | flops 8000000 | bytes 6000000 | tf_op jit(solution)/shard_map/second_step/pallas_call | solution.py:311
Async XLA Ops:
  0.0 1.2 %copy-start = (f32[2,16,64,128]{3,2,1,0:T(8,128)S(1)}, f32[2,16,64,128]{3,2,1,0:T(8,128)}, u32[]{:S(2)}) copy-start(f32[2,16,64,128]{3,2,1,0:T(8,128)} %noise_hi.1) | copy-start | bytes 3145732
  1.2 1.0 %copy-start.1 = (s32[16,64,128]{2,1,0:T(8,128)S(1)}, s32[16,64,128]{2,1,0:T(8,128)}, u32[]{:S(2)}) copy-start(s32[16,64,128]{2,1,0:T(8,128)} %mask.3) | copy-start | bytes 1572868
  2.3 1.0 %copy-start.3 = (f32[16,64,128]{2,1,0:T(8,128)S(1)}, f32[16,64,128]{2,1,0:T(8,128)}, u32[]{:S(2)}) copy-start(f32[16,64,128]{2,1,0:T(8,128)} %east.3) | copy-start | bytes 1572868
  3.3 1.0 %copy-start.5 = (f32[16,64,128]{2,1,0:T(8,128)S(1)}, f32[16,64,128]{2,1,0:T(8,128)}, u32[]{:S(2)}) copy-start(f32[16,64,128]{2,1,0:T(8,128)} %north.3) | copy-start | bytes 1572868
  4.6 8.4 %collective-permute-start = (f32[96,128]{1,0:T(8,128)S(1)}, f32[96,128]{1,0:T(8,128)S(1)}, u32[]{:S(2)}, u32[]{:S(2)}) collective-permute-start(f32[96,128]{1,0:T(8,128)S(1)} %get-tuple-element.16.own_b), channel_id=1, source_target_pairs={{0,32},{32,0},{64,96},{96,64},{128,160},{160,128},{192,224},{224,1... | collective-permute-start | bytes 147464 | tf_op jit(solution)/shard_map/ppermute | solution.py:281
  6.2 9.6 %collective-permute-start.1 = (f32[96,128]{1,0:T(8,128)S(1)}, f32[96,128]{1,0:T(8,128)S(1)}, u32[]{:S(2)}, u32[]{:S(2)}) collective-permute-start(f32[96,128]{1,0:T(8,128)S(1)} %get-tuple-element.17.own_a), channel_id=1, source_target_pairs={{32,64},{64,32},{96,128},{128,96},{160,192},{192,160},{224,255},{3... | collective-permute-start | bytes 147464 | tf_op jit(solution)/shard_map/ppermute | solution.py:282
  9.9 14.6 %copy-start.2 = (s32[16,64,128]{2,1,0:T(8,128)S(1)}, s32[16,64,128]{2,1,0:T(8,128)}, u32[]{:S(2)}) copy-start(s32[16,64,128]{2,1,0:T(8,128)} %mask.3) | copy-start | bytes 1572868
  10.0 14.6 %copy-start.4 = (f32[16,64,128]{2,1,0:T(8,128)S(1)}, f32[16,64,128]{2,1,0:T(8,128)}, u32[]{:S(2)}) copy-start(f32[16,64,128]{2,1,0:T(8,128)} %east.3) | copy-start | bytes 1572868
  10.0 14.6 %copy-start.6 = (f32[16,64,128]{2,1,0:T(8,128)S(1)}, f32[16,64,128]{2,1,0:T(8,128)}, u32[]{:S(2)}) copy-start(f32[16,64,128]{2,1,0:T(8,128)} %north.3) | copy-start | bytes 1572868
  16.1 6.8 %collective-permute-start.2 = (f32[72,128]{1,0:T(8,128)S(1)}, f32[72,128]{1,0:T(8,128)S(1)}, u32[]{:S(2)}, u32[]{:S(2)}) collective-permute-start(f32[72,128]{1,0:T(8,128)S(1)} %get-tuple-element.20), channel_id=1, source_target_pairs={{0,1},{1,0},{2,3},{3,2},{4,5},{5,4},{6,7},{7,6},{8,9},{9,8},{10,11... | collective-permute-start | bytes 110600 | tf_op jit(solution)/shard_map/ppermute | solution.py:308
  16.2 8.4 %collective-permute-start.3 = (f32[72,128]{1,0:T(8,128)S(1)}, f32[72,128]{1,0:T(8,128)S(1)}, u32[]{:S(2)}, u32[]{:S(2)}) collective-permute-start(f32[72,128]{1,0:T(8,128)S(1)} %get-tuple-element.21), channel_id=1, source_target_pairs={{0,31},{1,2},{2,1},{3,4},{4,3},{5,6},{6,5},{7,8},{8,7},{9,10},{10,... | collective-permute-start | bytes 110600 | tf_op jit(solution)/shard_map/ppermute | solution.py:309

commit v2 on v1

v2 whole, which is shorter than its diff:
```python
import jax
import jax.numpy as jnp
from jax import lax
from jax.experimental import pallas as pl
from jax.experimental.pallas import tpu as pltpu
from jax.sharding import PartitionSpec as P


LEVELS, ROWS, COLS = 16, 64, 128
PACKED = 72
NORTH, SOUTH = 64, 71
F32 = jnp.float32
VMEM = pl.BlockSpec(memory_space=pltpu.VMEM)
HBM = pl.BlockSpec(memory_space=pltpu.HBM)


def lanes(rows):
    return lax.broadcasted_iota(jnp.int32, (rows, COLS), 1)


def turned(x, shift):
    return pltpu.roll(x, shift % COLS if isinstance(shift, int) else shift, 1)


def slid(x, shift):
    return pltpu.roll(x, shift % x.shape[0], 0)


def edge_rows(noise, mask, east, north, out_b, out_a, noise_at, mask_at, east_at, north_at, sem):
    copies = []
    for k, (whole, part) in enumerate(((noise, noise_at), (mask, mask_at), (east, east_at), (north, north_at))):
        for end in range(2):
            span = pl.ds(end * (ROWS - 2), 2)
            source = whole.at[:, :, span, :] if k == 0 else whole.at[:, span, :]
            copies.append(pltpu.make_async_copy(source, part.at[end], sem.at[k, end]))
    for copy in copies:
        copy.start()
    lat = lax.axis_index("lat")
    top_block = lat == lax.axis_size("lat") - 1
    even = lax.rem(lat, 2) == 0
    lane = lanes(LEVELS)

    def lateral(u, east, west):
        return east * (turned(u, -1) - u) - west * (u - turned(u, 1))

    def inner_faces(east):
        return jnp.where(lane == COLS - 1, 0.0, east), jnp.where(lane == 0, 0.0, turned(east, 1))

    for copy in copies:
        copy.wait()
    mask_t = mask_at[1, :, 1, :].astype(F32)
    mask_t2 = mask_at[1, :, 0, :].astype(F32)
    mask_b = mask_at[0, :, 0, :].astype(F32)
    mask_b2 = mask_at[0, :, 1, :].astype(F32)
    full_t, full_b = east_at[1, :, 1, :], east_at[0, :, 0, :]
    east_t, west_t = inner_faces(full_t)
    east_b, west_b = inner_faces(full_b)
    south_t = north_at[1, :, 0, :]
    north_b = north_at[0, :, 0, :]
    top, bottom = [], []
    top_p, bottom_p = [], []
    for m in range(2):
        u = noise_at[1, m, :, 1, :] * mask_t
        v = noise_at[1, m, :, 0, :] * mask_t2
        top.append(u)
        top_p.append(mask_t * (u + lateral(u, east_t, west_t) - south_t * (u - v)))
        u = noise_at[0, m, :, 0, :] * mask_b
        v = noise_at[0, m, :, 1, :] * mask_b2
        bottom.append(u)
        bottom_p.append(mask_b * (u + lateral(u, east_b, west_b) + north_b * (v - u)))
    top += top_p + [north_at[1, :, 1, :] * mask_t, full_t * mask_t]
    bottom += bottom_p + [mask_b, full_b * mask_b]
    flip = jnp.where(top_block, COLS - 1 - lane, lane)
    for q in range(6):
        rows = pl.ds(q * LEVELS, LEVELS)
        out_b[rows, :] = jnp.where(even, top[q], bottom[q])
        crossed = jnp.take_along_axis(top[q], flip, axis=1)
        out_a[rows, :] = jnp.where(even, bottom[q], crossed)


CHUNK = 4


def first_step(
    noise, mask, east, north, out_u0, out_u1, out_values, out_east, out_north, out_mask, held_east, held_north, held_mask, sem
):
    out_u = (out_u0, out_u1)

    def copies(c):
        span = pl.ds(c * CHUNK, CHUNK)
        pairs = [(noise.at[0, span], out_u0.at[span]), (noise.at[1, span], out_u1.at[span])]
        pairs += [(mask.at[span], held_mask.at[span]), (east.at[span], held_east.at[span])]
        pairs += [(north.at[span], held_north.at[span])]
        return [pltpu.make_async_copy(a, b, sem.at[c, k]) for k, (a, b) in enumerate(pairs)]

    for c in range(LEVELS // CHUNK):
        for copy in copies(c):
            copy.start()
    lane = lanes(ROWS)
    row = lax.broadcasted_iota(jnp.int32, (ROWS, COLS), 0)
    group = lane // 4

    def level(l, carry):
        values, easts, norths, masks = carry
        k = held_mask[l].astype(F32)
        e_all = held_east[l]
        n_all = held_north[l]
        e = jnp.where(lane == COLS - 1, 0.0, e_all)
        w = jnp.where(lane == 0, 0.0, turned(e_all, 1))
        n = jnp.where(row == ROWS - 1, 0.0, n_all)
        s = jnp.where(row == 0, 0.0, slid(n_all, 1))
        here = group == l
        shift = 4 * l + 2
        easts = jnp.where(here, turned(e_all * k, shift), easts)
        norths = jnp.where(here, turned(n_all, shift), norths)
        masks = jnp.where(here, turned(k, shift), masks)
        for m in range(2):
            u = out_u[m][l] * k
            u_e, u_w = turned(u, -1), turned(u, 1)
            flux = e * (u_e - u) - w * (u - u_w)
            flux = flux + n * (slid(u, -1) - u) - s * (u - slid(u, 1))
            v = k * (u + flux)
            out_u[m][l] = v
            edges = jnp.where(lane == COLS - 2, u_e, jnp.where(lane == 1, u_w, v))
            values = jnp.where(group == m * 16 + l, turned(edges, 64 * m + shift), values)
        return values, easts, norths, masks

    carry = (jnp.zeros((ROWS, COLS), F32),) * 4
    for c in range(LEVELS // CHUNK):
        for copy in copies(c):
            copy.wait()
        carry = lax.fori_loop(c * CHUNK, (c + 1) * CHUNK, level, carry)
    values, easts, norths, masks = carry
    out_values[...] = values
    for out, x in ((out_east, easts), (out_north, norths), (out_mask, masks)):
        out[...] = jnp.where(lane < 64, x, turned(x, 64))


def join_rows(
    own_b, own_a, got_b, got_a, values, easts, norths, masks,
    send_1, send_2, out_values, out_east, out_north, out_mask, out_rows, south, north, side
):
    lat = lax.axis_index("lat")
    top_block = lat == lax.axis_size("lat") - 1
    even = lax.rem(lat, 2) == 0
    even_lon = lax.rem(lax.axis_index("lon"), 2) == 0

    def part(q):
        rows = pl.ds(q * LEVELS, LEVELS)
        ob, oa, gb, ga = own_b[rows, :], own_a[rows, :], got_b[rows, :], got_a[rows, :]
        return ob, oa, jnp.where(even, gb, ga), jnp.where(even, ga, gb)

    flip = COLS - 1 - lanes(LEVELS)

    def own(q):
        ob, oa, _, _ = part(q)
        back = jnp.where(top_block, jnp.take_along_axis(oa, flip, axis=1), oa)
        return jnp.where(even, ob, back), jnp.where(even, oa, ob)

    def put(ref, half, slots, x):
        for j in slots:
            ref[pl.ds(half * 64 + j, LEVELS, stride=4), :] = x

    own_n, own_k = own(4)
    _, _, far_n, far_s = part(4)
    ghost_n = jnp.where(top_block, far_n, own_n * far_n)
    for m in range(2):
        own_t, own_bot = own(m)
        _, _, up, down = part(m)
        _, _, up_p, down_p = part(2 + m)
        gain_s = own_k * far_s * (down - own_bot)
        gain_n = own_n * (up - own_t)
        out_rows[pl.ds(m * LEVELS, LEVELS), :] = gain_s
        out_rows[pl.ds((2 + m) * LEVELS, LEVELS), :] = gain_n
        out_rows[pl.ds((4 + m) * LEVELS, LEVELS), :] = down_p - far_s * (down - own_bot)
        out_rows[pl.ds((6 + m) * LEVELS, LEVELS), :] = up_p - ghost_n * (up - own_t)
        put(south, m, (0, 3), down)
        put(south, m, (1, 2), gain_s)
        put(north, m, (0, 3), up)
        put(north, m, (1, 2), gain_n)
    out_rows[pl.ds(8 * LEVELS, LEVELS), :] = far_s
    _, _, up_e, down_e = part(5)
    put(side, 0, (0, 1), down_e)
    put(side, 0, (2, 3), far_s)
    put(side, 1, (0, 1, 2, 3), up_e)

    lane1 = lanes(1)
    slot1 = lax.rem(lane1, 4)
    turned_s = jnp.transpose(south[...])
    turned_n = jnp.transpose(north[...])
    turned_c = jnp.transpose(side[...])
    row_s = jnp.where(slot1 >= 2, turned_s[0:1, :], turned_s[COLS - 1 : COLS, :])
    row_n = jnp.where(slot1 >= 2, turned_n[0:1, :], turned_n[COLS - 1 : COLS, :])
    inner = (slot1 == 1) | (slot1 == 2)
    low_half = lane1 < 64
    first_c, last_c = turned_c[0:1, :], turned_c[COLS - 1 : COLS, :]
    face_s = jnp.where(low_half, last_c, turned(last_c, 64))
    coef_s = jnp.where(slot1 == 1, turned(last_c, -1), first_c)
    coef_s = jnp.where(low_half, coef_s, turned(coef_s, 64))
    face_n = jnp.where(low_half, turned(last_c, 64), last_c)
    mirrored = jnp.where(low_half, turned(first_c, 64), first_c)

    def extend(out, x, north_row, south_row):
        out[0:ROWS, :] = x[...]
        out[ROWS:PACKED, :] = jnp.zeros((PACKED - ROWS, COLS), F32)
        out[NORTH : NORTH + 1, :] = north_row
        out[SOUTH : SOUTH + 1, :] = south_row

    one = jnp.ones((1, COLS), F32)
    extend(out_values, values, row_n, row_s)
    out_values[0:1, :] = values[0:1, :] + jnp.where(inner, row_s, 0.0)
    out_values[ROWS - 1 : ROWS, :] = values[ROWS - 1 : ROWS, :] + jnp.where(inner, row_n, 0.0)
    extend(out_east, easts, jnp.where(top_block, one, face_n), face_s)
    extend(out_mask, masks, jnp.where(top_block, mirrored, one), one)
    extend(out_north, norths, jnp.zeros((1, COLS), F32), coef_s)
    slot = lax.rem(lanes(PACKED), 4)
    x = out_values[...]
    eastward = jnp.where(slot >= 2, turned(x, 2), out_east[...])
    westward = jnp.where(slot < 2, turned(x, -2), out_mask[...])
    send_1[...] = jnp.where(even_lon, eastward, westward)
    send_2[...] = jnp.where(even_lon, westward, eastward)


def second_step(u1_0, u1_1, mask, east, north, rows, out):
    u1 = (u1_0, u1_1)
    lane = lanes(ROWS)
    row = lax.broadcasted_iota(jnp.int32, (ROWS, COLS), 0)

    def line(q, l):
        return rows[pl.ds(q * LEVELS + l, 1), :]

    def level(l, carry):
        k = mask[l].astype(F32)
        e_all = east[l]
        n = north[l]
        e = jnp.where(lane == COLS - 1, 0.0, e_all)
        w = jnp.where(lane == 0, 0.0, turned(e_all, 1))
        s = jnp.where(row == 0, line(8, l), slid(n, 1))
        for m in range(2):
            u = u1[m][l]
            u = jnp.where(row == 0, u + line(m, l), u)
            u = jnp.where(row == ROWS - 1, u + line(2 + m, l), u)
            u_n = jnp.where(row == ROWS - 1, line(6 + m, l), slid(u, -1))
            u_s = jnp.where(row == 0, line(4 + m, l), slid(u, 1))
            flux = e * (turned(u, -1) - u) - w * (u - turned(u, 1))
            flux = flux + n * (u_n - u) - s * (u - u_s)
            out[m, l] = k * (u + flux)
        return carry

    lax.fori_loop(0, LEVELS, level, 0)


def join_columns(u2, got_1, got_2, values, easts, norths, masks, out, gain, held, sem):
    even_lon = lax.rem(lax.axis_index("lon"), 2) == 0
    slot = lax.rem(lanes(PACKED), 4)
    is_east = slot == 1
    inner = is_east | (slot == 2)
    from_east = jnp.where(even_lon, got_1[...], got_2[...])
    from_west = jnp.where(even_lon, got_2[...], got_1[...])
    x, e, n, k = values[...], easts[...], norths[...], masks[...]
    own_0 = jnp.where(is_east, turned(x, 1), turned(x, -1))
    ghost_0 = jnp.where(is_east, from_east, from_west)
    ghost_1 = jnp.where(is_east, turned(from_east, 1), turned(from_west, -1))
    face = jnp.where(is_east, e * turned(from_east, -1), k * turned(from_west, 1))
    d = jnp.where(inner, face * (ghost_0 - own_0), 0.0)
    inside = jnp.where(is_east, turned(e, 1), e)
    s = slid(n, 1)
    change = d * (1.0 - inside - n - s) + face * (ghost_1 - x - d - d) + n * slid(d, -1) + s * slid(d, 1)
    beside = inside * d
    beside = jnp.where(slot == 0, turned(beside, -1), turned(beside, 1))
    gain[...] = k * jnp.where(inner, change, beside)

    lane = lanes(ROWS)
    edge = (lane < 2) | (lane >= COLS - 2)

    def copy(m, c):
        span = pl.ds(c * CHUNK, CHUNK)
        return pltpu.make_async_copy(held.at[m, span], out.at[m, span], sem.at[m, c])

    for c in range(LEVELS // CHUNK):
        for m in range(2):
            for l in range(c * CHUNK, (c + 1) * CHUNK):
                change = turned(gain[0:ROWS, :], 126 - 64 * m - 4 * l)
                held[m, l] = u2[m, l] + jnp.where(edge, change, 0.0)
            copy(m, c).start()
    for c in range(LEVELS // CHUNK):
        for m in range(2):
            copy(m, c).wait()


def struct(*shape):
    return jax.ShapeDtypeStruct(shape, F32)


def kernel(body, name, inputs, outputs, us, scratch=(), space=VMEM, limit=16):
    return pl.pallas_call(
        body,
        in_specs=[space] * inputs,
        out_specs=[VMEM if body is not join_columns else HBM] * len(outputs),
        out_shape=outputs,
        scratch_shapes=list(scratch),
        compiler_params=pltpu.CompilerParams(vmem_limit_bytes=limit * 1024 * 1024),
        cost_estimate=pl.CostEstimate(flops=int(us * 4e6), bytes_accessed=int(us * 3e6), transcendentals=0),
        name=name,
    )


def local(noise, land_mask, east_coef, north_coef):
    n_lat, n_lon = lax.axis_size("lat"), lax.axis_size("lon")
    message = struct(6 * LEVELS, COLS)
    ends = pltpu.VMEM((2, LEVELS, 2, COLS), F32)
    scratch = [
        pltpu.VMEM((2, 2, LEVELS, 2, COLS), F32),
        pltpu.VMEM((2, LEVELS, 2, COLS), jnp.int32),
        ends,
        ends,
        pltpu.SemaphoreType.DMA((4, 2)),
    ]
    send_b, send_a = kernel(edge_rows, "edge_rows", 4, [message] * 2, 1, scratch, HBM, 63)(
        noise, land_mask, east_coef, north_coef
    )

    route_b = [(i, i ^ 1) for i in range(n_lat)]
    route_a = []
    for k in range(n_lon):
        for i in range(1, n_lat - 1):
            route_a.append((i * n_lon + k, (((i - 1) ^ 1) + 1) * n_lon + k))
        route_a.append(((n_lat - 1) * n_lon + k, n_lat * n_lon - 1 - k))
    got_a = lax.ppermute(send_a, ("lat", "lon"), route_a)
    got_b = lax.ppermute(send_b, "lat", route_b)

    whole, plane, packed = struct(2, LEVELS, ROWS, COLS), struct(ROWS, COLS), struct(PACKED, COLS)
    coef, levels = struct(LEVELS, ROWS, COLS), jax.ShapeDtypeStruct((LEVELS, ROWS, COLS), jnp.int32)
    outs = [coef] * 2 + [plane] * 4 + [coef] * 2 + [levels]
    scratch = [pltpu.SemaphoreType.DMA((LEVELS // CHUNK, 5))]
    u1_0, u1_1, *columns, east, north, mask = kernel(first_step, "first_step", 4, outs, 2, scratch, HBM, 51)(
        noise, land_mask, east_coef, north_coef
    )
    square = pltpu.VMEM((COLS, COLS), F32)
    send_1, send_2, *columns, rows = kernel(
        join_rows, "join_rows", 8, [packed] * 6 + [struct(9 * LEVELS, COLS)], 1, [square] * 3
    )(send_b, send_a, got_b, got_a, *columns)

    route_1 = [(k, k ^ 1) for k in range(n_lon)]
    route_2 = [(k, (((k + n_lon - 1) % n_lon ^ 1) + 1) % n_lon) for k in range(n_lon)]
    got_2 = lax.ppermute(send_2, "lon", route_2)
    got_1 = lax.ppermute(send_1, "lon", route_1)

    (u2,) = kernel(second_step, "second_step", 6, [whole], 2)(u1_0, u1_1, mask, east, north, rows)
    scratch = [pltpu.VMEM((PACKED, COLS), F32), pltpu.VMEM(whole.shape, F32), pltpu.SemaphoreType.DMA((2, LEVELS // CHUNK))]
    return kernel(join_columns, "join_columns", 7, [whole], 1, scratch)(u2, got_1, got_2, *columns)[0]


def solution(mesh):
    return jax.shard_map(
        local,
        mesh=mesh,
        in_specs=(
            P(None, None, "lat", "lon"),
            P(None, "lat", "lon"),
            P(None, "lat", "lon"),
            P(None, "lat", "lon"),
        ),
        out_specs=P(None, None, "lat", "lon"),
        check_vma=False,
    )
```

time: 29 us -> 23.8 us (0.82)
  local copies, waits for them, and re-layouts: 4.37 us -> 0.01 us
  waiting for transfers between devices: 4.42 us -> 1.51 us
  Pallas kernels: 7.76 us -> 9.79 us
    unnamed x14 -> x4, local copies, waits for them, and re-layouts: 4.37 us -> 0.01 us
    pallas_call x4 -> x5, Pallas kernels: 7.76 us -> 9.79 us  [the longest x1 4.5 us: local(): kernel(first_step, 'first_step', 4, outs, 2, scratch, HBM, 51)]
    ppermute x1, waiting for transfers between devices: 1.64 us -> 0.01 us  [local(): got_2 = lax.ppermute(send_2, 'lon', route_2)]
    ppermute x1, waiting for transfers between devices: 2.78 us -> 1.51 us  [local(): got_a = lax.ppermute(send_a, ('lat', 'lon'), route_a)]
  transfers between devices with their start and end apart: 4 -> 4, of which waited for: 2 -> 1; matrix products, arithmetic and copies ran while one was open for 0% -> 0% of each run, Pallas kernels for 10% -> 27%
where the time goes in v2:
time: 23.8 us; the launch traced here: 23.6 us
  starting transfers between devices  12.2 us (51%)
  Pallas kernels  9.79 us (41%)
  waiting for transfers between devices  1.51 us (6%)
    ppermute x1, starting transfers between devices, local(): got_2 = lax.ppermute(send_2, 'lon', route_2)  6.68 us
    pallas_call x1, Pallas kernels, local(): kernel(first_step, 'first_step', 4, outs, 2, scratch, HBM, 51)  4.5 us
    ppermute x1, starting transfers between devices, local(): got_a = lax.ppermute(send_a, ('lat', 'lon'), route_a)  3.9 us
    pallas_call x1, Pallas kernels, local(): kernel(second_step, 'second_step', 6, [whole], 2)  1.98 us
    pallas_call x1, Pallas kernels, local(): kernel(edge_rows, 'edge_rows', 4, [message] * 2, 1, scratch, HBM, 63)  1.71 us
    ppermute x1, starting transfers between devices, local(): got_b = lax.ppermute(send_b, 'lat', route_b)  1.58 us
    ppermute x1, waiting for transfers between devices, local(): got_a = lax.ppermute(send_a, ('lat', 'lon'), route_a)  1.51 us
    pallas_call x1, Pallas kernels, local(): kernel(join_columns, 'join_columns', 7, [whole], 1, scratch)  1.34 us
  transfers between devices with their start and end apart: 4, of which 1 were waited for; matrix products, arithmetic and copies ran while one was open for 0% of the time, Pallas kernels for 27%

profile of v2, /device:TPU:16, one launch (start us, length us, event | category | flops | bytes accessed | tf_op | source)
XLA Modules:
  0.0 23.6 jit_solution(7021199167994256885)
XLA Ops:
  0.0 1.7 %edge_rows.1 = (f32[96,128]{1,0:T(8,128)}, f32[96,128]{1,0:T(8,128)}) custom-call(f32[2,16,64,128]{3,2,1,0:T(8,128)} %noise.3, s32[16,64,128]{2,1,0:T(8,128)} %mask.3, f32[16,64,128]{2,1,0:T(8,128)} %east.3, f32[16,64,128]{2,1,0:T(8,128)} %north.3), custom_call_target="tpu_custom_call" | custom-call | flops 4000000 | bytes 3000000 | tf_op jit(solution)/shard_map/edge_rows/pallas_call | solution.py:319
  1.7 1.6 %collective-permute-start = (f32[96,128]{1,0:T(8,128)}, f32[96,128]{1,0:T(8,128)S(1)}, u32[]{:S(2)}, u32[]{:S(2)}) collective-permute-start(f32[96,128]{1,0:T(8,128)} %get-tuple-element.28.own_b), channel_id=1, source_target_pairs={{0,32},{32,0},{64,96},{96,64},{128,160},{160,128},{192,224},{224,1... | collective-permute-start | bytes 147464 | tf_op jit(solution)/shard_map/ppermute | solution.py:330
  3.3 0.0 copy-start
  3.3 0.0 copy-start.1
  3.3 3.9 %collective-permute-start.1 = (f32[96,128]{1,0:T(8,128)}, f32[96,128]{1,0:T(8,128)S(1)}, u32[]{:S(2)}, u32[]{:S(2)}) collective-permute-start(f32[96,128]{1,0:T(8,128)} %get-tuple-element.29.own_a), channel_id=1, source_target_pairs={{32,64},{64,32},{96,128},{128,96},{160,192},{192,160},{224,255},{3... | collective-permute-start | bytes 147464 | tf_op jit(solution)/shard_map/ppermute | solution.py:329
  7.2 4.5 %first_step.1 = (f32[16,64,128]{2,1,0:T(8,128)S(1)}, f32[16,64,128]{2,1,0:T(8,128)S(1)}, f32[64,128]{1,0:T(8,128)S(1)}, f32[64,128]{1,0:T(8,128)S(1)}, f32[64,12...) custom-call(f32[2,16,64,128]{3,2,1,0:T(8,128)} %noise.3, ...), custom_call_target="tpu_custom_call" | custom-call | flops 8000000 | bytes 6000000 | tf_op jit(solution)/shard_map/first_step/pallas_call | solution.py:336
  11.7 0.0 collective-permute-done.got_b
  11.7 1.5 %collective-permute-done.1.got_a = f32[96,128]{1,0:T(8,128)S(1)} collective-permute-done((f32[96,128]{1,0:T(8,128)}, f32[96,128]{1,0:T(8,128)S(1)}, u32[]{:S(2)}, u32[]{:S(2)}) %collective-permute-start.1) | collective-permute-done | bytes 49184 | tf_op jit(solution)/shard_map/ppermute | solution.py:329
  13.2 0.0 copy-done
  13.2 0.0 copy-done.1
  13.2 0.3 %join_rows.1 = (f32[72,128]{1,0:T(8,128)S(1)}, f32[72,128]{1,0:T(8,128)S(1)}, f32[72,128]{1,0:T(8,128)S(1)}, f32[72,128]{1,0:T(8,128)S(1)}, f32[72,128]{1,0:T(8,...) custom-call(f32[96,128]{1,0:T(8,128)S(1)} %copy-done, f32[96,128]{1,0:T(8,128)S(1)} %copy-done.1, ...), custom_call_target="tpu_custom_call" | custom-call | flops 4000000 | bytes 3000000 | tf_op jit(solution)/shard_map/join_rows/pallas_call | solution.py:340
  13.5 0.1 collective-permute-start.2
  13.6 6.7 %collective-permute-start.3 = (f32[72,128]{1,0:T(8,128)S(1)}, f32[72,128]{1,0:T(8,128)S(1)}, u32[]{:S(2)}, u32[]{:S(2)}) collective-permute-start(f32[72,128]{1,0:T(8,128)S(1)} %get-tuple-element.36), channel_id=1, source_target_pairs={{0,31},{1,2},{2,1},{3,4},{4,3},{5,6},{6,5},{7,8},{8,7},{9,10},{10,... | collective-permute-start | bytes 110600 | tf_op jit(solution)/shard_map/ppermute | solution.py:346
  20.2 2.0 %second_step.1.u2 = f32[2,16,64,128]{3,2,1,0:T(8,128)S(1)} custom-call(f32[16,64,128]{2,1,0:T(8,128)S(1)} %get-tuple-element.23.u1_0, f32[16,64,128]{2,1,0:T(8,128)S(1)} %get-tuple-element.24.u1_1, s32[16,64,128]{2,1,0:T(8,128)S(1)} %get-tuple-element.25.mask, f32[16,64,128]{2,1,0:T(8,128)S(1)} %get-tuple-element.26.east, ...), custom_call_target="tpu_custom_call" | custom-call | flops 8000000 | bytes 6000000 | tf_op jit(solution)/shard_map/second_step/pallas_call | solution.py:349
  22.2 0.0 collective-permute-done.2.got_1
  22.2 0.0 collective-permute-done.3.got_2
  22.3 1.3 %join_columns.1 = f32[2,16,64,128]{3,2,1,0:T(8,128)} custom-call(f32[2,16,64,128]{3,2,1,0:T(8,128)S(1)} %second_step.1.u2, f32[72,128]{1,0:T(8,128)S(1)} %collective-permute-done.2.got_1, f32[72,128]{1,0:T(8,128)S(1)} %collective-permute-done.3.got_2, f32[72,128]{1,0:T(8,128)S(1)} %get-tuple-element.37.values, f32[72,128]{1,0:T(8,128)S(1)} %get-tuple-element.38.easts, ...), custom_call_target="tpu_custom_call" | custom-call | flops 4000000 | bytes 3000000 | tf_op jit(solution)/shard_map/join_columns/pallas_call | solution.py:351
Async XLA Ops:
  1.7 10.0 %collective-permute-start = (f32[96,128]{1,0:T(8,128)}, f32[96,128]{1,0:T(8,128)S(1)}, u32[]{:S(2)}, u32[]{:S(2)}) collective-permute-start(f32[96,128]{1,0:T(8,128)} %get-tuple-element.28.own_b), channel_id=1, source_target_pairs={{0,32},{32,0},{64,96},{96,64},{128,160},{160,128},{192,224},{224,1... | collective-permute-start | bytes 147464 | tf_op jit(solution)/shard_map/ppermute | solution.py:330
  3.3 9.9 %copy-start = (f32[96,128]{1,0:T(8,128)S(1)}, f32[96,128]{1,0:T(8,128)}, u32[]{:S(2)}) copy-start(f32[96,128]{1,0:T(8,128)} %get-tuple-element.28.own_b) | copy-start | bytes 147460
  3.3 9.9 %copy-start.1 = (f32[96,128]{1,0:T(8,128)S(1)}, f32[96,128]{1,0:T(8,128)}, u32[]{:S(2)}) copy-start(f32[96,128]{1,0:T(8,128)} %get-tuple-element.29.own_a) | copy-start | bytes 147460
  3.3 9.9 %collective-permute-start.1 = (f32[96,128]{1,0:T(8,128)}, f32[96,128]{1,0:T(8,128)S(1)}, u32[]{:S(2)}, u32[]{:S(2)}) collective-permute-start(f32[96,128]{1,0:T(8,128)} %get-tuple-element.29.own_a), channel_id=1, source_target_pairs={{32,64},{64,32},{96,128},{128,96},{160,192},{192,160},{224,255},{3... | collective-permute-start | bytes 147464 | tf_op jit(solution)/shard_map/ppermute | solution.py:329
  13.5 8.7 %collective-permute-start.2 = (f32[72,128]{1,0:T(8,128)S(1)}, f32[72,128]{1,0:T(8,128)S(1)}, u32[]{:S(2)}, u32[]{:S(2)}) collective-permute-start(f32[72,128]{1,0:T(8,128)S(1)} %get-tuple-element.35), channel_id=1, source_target_pairs={{0,1},{1,0},{2,3},{3,2},{4,5},{5,4},{6,7},{7,6},{8,9},{9,8},{10,11... | collective-permute-start | bytes 110600 | tf_op jit(solution)/shard_map/ppermute | solution.py:347
  13.6 8.7 %collective-permute-start.3 = (f32[72,128]{1,0:T(8,128)S(1)}, f32[72,128]{1,0:T(8,128)S(1)}, u32[]{:S(2)}, u32[]{:S(2)}) collective-permute-start(f32[72,128]{1,0:T(8,128)S(1)} %get-tuple-element.36), channel_id=1, source_target_pairs={{0,31},{1,2},{2,1},{3,4},{4,3},{5,6},{6,5},{7,8},{8,7},{9,10},{10,... | collective-permute-start | bytes 110600 | tf_op jit(solution)/shard_map/ppermute | solution.py:346

commit v3 on v2

--- a/solution.py
+++ b/solution.py
@@ -26,7 +26,7 @@
     return pltpu.roll(x, shift % x.shape[0], 0)
 
 
-def edge_rows(noise, mask, east, north, out_b, out_a, noise_at, mask_at, east_at, north_at, sem):
+def edge_rows(noise, mask, east, north, out_a, out_b, noise_at, mask_at, east_at, north_at, sem):
     copies = []
     for k, (whole, part) in enumerate(((noise, noise_at), (mask, mask_at), (east, east_at), (north, north_at))):
         for end in range(2):
@@ -79,29 +79,32 @@
 
 
 CHUNK = 4
+FETCH = 4
 
 
 def first_step(
-    noise, mask, east, north, out_u0, out_u1, out_values, out_east, out_north, out_mask, held_east, held_north, held_mask, sem
+    noise, mask, east, north, out_u0, out_u1, out_values, out_east, out_north, out_mask, held_east, held_north, held_mask, edges, sem
 ):
     out_u = (out_u0, out_u1)
 
     def copies(c):
-        span = pl.ds(c * CHUNK, CHUNK)
+        span = pl.ds(c * FETCH, FETCH)
         pairs = [(noise.at[0, span], out_u0.at[span]), (noise.at[1, span], out_u1.at[span])]
         pairs += [(mask.at[span], held_mask.at[span]), (east.at[span], held_east.at[span])]
         pairs += [(north.at[span], held_north.at[span])]
         return [pltpu.make_async_copy(a, b, sem.at[c, k]) for k, (a, b) in enumerate(pairs)]
 
-    for c in range(LEVELS // CHUNK):
+    for c in range(min(LEVELS // FETCH, 99)):
         for copy in copies(c):
             copy.start()
     lane = lanes(ROWS)
     row = lax.broadcasted_iota(jnp.int32, (ROWS, COLS), 0)
     group = lane // 4
 
-    def level(l, carry):
-        values, easts, norths, masks = carry
+    def place(out, x, at):
+        pltpu.store(out, turned(x, 4 * at + 2), mask=group == at)
+
+    def level(l):
         k = held_mask[l].astype(F32)
         e_all = held_east[l]
         n_all = held_north[l]
@@ -109,11 +112,6 @@
         w = jnp.where(lane == 0, 0.0, turned(e_all, 1))
         n = jnp.where(row == ROWS - 1, 0.0, n_all)
         s = jnp.where(row == 0, 0.0, slid(n_all, 1))
-        here = group == l
-        shift = 4 * l + 2
-        easts = jnp.where(here, turned(e_all * k, shift), easts)
-        norths = jnp.where(here, turned(n_all, shift), norths)
-        masks = jnp.where(here, turned(k, shift), masks)
         for m in range(2):
             u = out_u[m][l] * k
             u_e, u_w = turned(u, -1), turned(u, 1)
@@ -121,24 +119,27 @@
             flux = flux + n * (slid(u, -1) - u) - s * (u - slid(u, 1))
             v = k * (u + flux)
             out_u[m][l] = v
-            edges = jnp.where(lane == COLS - 2, u_e, jnp.where(lane == 1, u_w, v))
-            values = jnp.where(group == m * 16 + l, turned(edges, 64 * m + shift), values)
-        return values, easts, norths, masks
-
-    carry = (jnp.zeros((ROWS, COLS), F32),) * 4
-    for c in range(LEVELS // CHUNK):
+            edges[m * LEVELS + l] = jnp.where(lane == COLS - 2, u_e, jnp.where(lane == 1, u_w, v))
+
+    for c in range(LEVELS // FETCH):
         for copy in copies(c):
             copy.wait()
-        carry = lax.fori_loop(c * CHUNK, (c + 1) * CHUNK, level, carry)
-    values, easts, norths, masks = carry
-    out_values[...] = values
-    for out, x in ((out_east, easts), (out_north, norths), (out_mask, masks)):
-        out[...] = jnp.where(lane < 64, x, turned(x, 64))
+        for l in range(c * FETCH, (c + 1) * FETCH):
+            level(l)
+    for l in range(LEVELS):
+        k = held_mask[l].astype(F32)
+        place(out_east, held_east[l] * k, l)
+        place(out_north, held_north[l], l)
+        place(out_mask, k, l)
+        for m in range(2):
+            place(out_values, edges[m * LEVELS + l], m * LEVELS + l)
+    for out in (out_east, out_north, out_mask):
+        out[...] = jnp.where(lane < 64, out[...], turned(out[...], 64))
 
 
 def join_rows(
-    own_b, own_a, got_b, got_a, values, easts, norths, masks,
-    send_1, send_2, out_values, out_east, out_north, out_mask, out_rows, south, north, side
+    own_a, own_b, got_a, got_b, values, easts, norths, masks,
+    send_2, send_1, out_values, out_east, out_north, out_mask, out_rows, south, north, side
 ):
     lat = lax.axis_index("lat")
     top_block = lat == lax.axis_size("lat") - 1
@@ -229,7 +230,7 @@
     def line(q, l):
         return rows[pl.ds(q * LEVELS + l, 1), :]
 
-    def level(l, carry):
+    def level(l):
         k = mask[l].astype(F32)
         e_all = east[l]
         n = north[l]
@@ -245,12 +246,12 @@
             flux = e * (turned(u, -1) - u) - w * (u - turned(u, 1))
             flux = flux + n * (u_n - u) - s * (u - u_s)
             out[m, l] = k * (u + flux)
-        return carry
-
-    lax.fori_loop(0, LEVELS, level, 0)
-
-
-def join_columns(u2, got_1, got_2, values, easts, norths, masks, out, gain, held, sem):
+
+    for l in range(LEVELS):
+        level(l)
+
+
+def join_columns(u2, got_2, got_1, values, easts, norths, masks, out, gain, held, sem):
     even_lon = lax.rem(lax.axis_index("lon"), 2) == 0
     slot = lax.rem(lanes(PACKED), 4)
     is_east = slot == 1
@@ -316,7 +317,7 @@
         ends,
         pltpu.SemaphoreType.DMA((4, 2)),
     ]
-    send_b, send_a = kernel(edge_rows, "edge_rows", 4, [message] * 2, 1, scratch, HBM, 63)(
+    send_a, send_b = kernel(edge_rows, "edge_rows", 4, [message] * 2, 1, scratch, HBM, 63)(
         noise, land_mask, east_coef, north_coef
     )
 
@@ -332,14 +333,14 @@
     whole, plane, packed = struct(2, LEVELS, ROWS, COLS), struct(ROWS, COLS), struct(PACKED, COLS)
     coef, levels = struct(LEVELS, ROWS, COLS), jax.ShapeDtypeStruct((LEVELS, ROWS, COLS), jnp.int32)
     outs = [coef] * 2 + [plane] * 4 + [coef] * 2 + [levels]
-    scratch = [pltpu.SemaphoreType.DMA((LEVELS // CHUNK, 5))]
+    scratch = [pltpu.VMEM((2 * LEVELS, ROWS, COLS), F32), pltpu.SemaphoreType.DMA((LEVELS // FETCH, 5))]
     u1_0, u1_1, *columns, east, north, mask = kernel(first_step, "first_step", 4, outs, 2, scratch, HBM, 51)(
         noise, land_mask, east_coef, north_coef
     )
     square = pltpu.VMEM((COLS, COLS), F32)
-    send_1, send_2, *columns, rows = kernel(
+    send_2, send_1, *columns, rows = kernel(
         join_rows, "join_rows", 8, [packed] * 6 + [struct(9 * LEVELS, COLS)], 1, [square] * 3
-    )(send_b, send_a, got_b, got_a, *columns)
+    )(send_a, send_b, got_a, got_b, *columns)
 
     route_1 = [(k, k ^ 1) for k in range(n_lon)]
     route_2 = [(k, (((k + n_lon - 1) % n_lon ^ 1) + 1) % n_lon) for k in range(n_lon)]
@@ -348,7 +349,7 @@
 
     (u2,) = kernel(second_step, "second_step", 6, [whole], 2)(u1_0, u1_1, mask, east, north, rows)
     scratch = [pltpu.VMEM((PACKED, COLS), F32), pltpu.VMEM(whole.shape, F32), pltpu.SemaphoreType.DMA((2, LEVELS // CHUNK))]
-    return kernel(join_columns, "join_columns", 7, [whole], 1, scratch)(u2, got_1, got_2, *columns)[0]
+    return kernel(join_columns, "join_columns", 7, [whole], 1, scratch)(u2, got_2, got_1, *columns)[0]
 
 
 def solution(mesh):

time: 23.8 us -> 21.7 us (0.912)
  the two profiles are of different devices: /device:TPU:16 before, /device:TPU:22 now
where the time goes in v3:
time: 21.7 us; the launch traced here: 21.5 us
  starting transfers between devices  10.1 us (47%)
  Pallas kernels  7.32 us (34%)
  waiting for transfers between devices  3.98 us (18%)
    ppermute x1, starting transfers between devices, local(): got_a = lax.ppermute(send_a, ('lat', 'lon'), route_a)  7.92 us
    pallas_call x1, Pallas kernels, local(): kernel(first_step, 'first_step', 4, outs, 2, scratch, HBM, 51)  3.16 us
    ppermute x1, waiting for transfers between devices, local(): got_2 = lax.ppermute(send_2, 'lon', route_2)  2.63 us
    ppermute x1, starting transfers between devices, local(): got_2 = lax.ppermute(send_2, 'lon', route_2)  2.03 us
    pallas_call x1, Pallas kernels, local(): kernel(edge_rows, 'edge_rows', 4, [message] * 2, 1, scratch, HBM, 63)  1.72 us
    ppermute x1, waiting for transfers between devices, local(): got_b = lax.ppermute(send_b, 'lat', route_b)  1.34 us
    pallas_call x1, Pallas kernels, local(): kernel(join_columns, 'join_columns', 7, [whole], 1, scratch)  1.34 us
    pallas_call x1, Pallas kernels, local(): kernel(second_step, 'second_step', 6, [whole], 2)  0.83 us
  transfers between devices with their start and end apart: 4, of which 2 were waited for; matrix products, arithmetic and copies ran while one was open for 0% of the time, Pallas kernels for 19%

profile of v3, /device:TPU:22, one launch (start us, length us, event | category | flops | bytes accessed | tf_op | source)
XLA Modules:
  0.0 21.5 jit_solution(10201937959937023061)
XLA Ops:
  0.0 1.7 %edge_rows.1 = (f32[96,128]{1,0:T(8,128)}, f32[96,128]{1,0:T(8,128)}) custom-call(f32[2,16,64,128]{3,2,1,0:T(8,128)} %noise.3, s32[16,64,128]{2,1,0:T(8,128)} %mask.3, f32[16,64,128]{2,1,0:T(8,128)} %east.3, f32[16,64,128]{2,1,0:T(8,128)} %north.3), custom_call_target="tpu_custom_call" | custom-call | flops 4000000 | bytes 3000000 | tf_op jit(solution)/shard_map/edge_rows/pallas_call | solution.py:320
  1.7 7.9 %collective-permute-start = (f32[96,128]{1,0:T(8,128)}, f32[96,128]{1,0:T(8,128)S(1)}, u32[]{:S(2)}, u32[]{:S(2)}) collective-permute-start(f32[96,128]{1,0:T(8,128)} %get-tuple-element.28.own_a), channel_id=1, source_target_pairs={{32,64},{64,32},{96,128},{128,96},{160,192},{192,160},{224,255},{3... | collective-permute-start | bytes 147464 | tf_op jit(solution)/shard_map/ppermute | solution.py:330
  9.7 0.0 copy-start
  9.7 0.0 copy-start.1
  9.7 0.1 collective-permute-start.1
  9.8 3.2 %first_step.1 = (f32[16,64,128]{2,1,0:T(8,128)S(1)}, f32[16,64,128]{2,1,0:T(8,128)S(1)}, f32[64,128]{1,0:T(8,128)S(1)}, f32[64,128]{1,0:T(8,128)S(1)}, f32[64,12...) custom-call(f32[2,16,64,128]{3,2,1,0:T(8,128)} %noise.3, ...), custom_call_target="tpu_custom_call" | custom-call | flops 8000000 | bytes 6000000 | tf_op jit(solution)/shard_map/first_step/pallas_call | solution.py:337
  12.9 0.0 collective-permute-done.got_a
  13.0 1.3 %collective-permute-done.1.got_b = f32[96,128]{1,0:T(8,128)S(1)} collective-permute-done((f32[96,128]{1,0:T(8,128)}, f32[96,128]{1,0:T(8,128)S(1)}, u32[]{:S(2)}, u32[]{:S(2)}) %collective-permute-start.1) | collective-permute-done | bytes 49184 | tf_op jit(solution)/shard_map/ppermute | solution.py:331
  14.3 0.0 copy-done
  14.3 0.0 copy-done.1
  14.3 0.3 %join_rows.1 = (f32[72,128]{1,0:T(8,128)S(1)}, f32[72,128]{1,0:T(8,128)S(1)}, f32[72,128]{1,0:T(8,128)S(1)}, f32[72,128]{1,0:T(8,128)S(1)}, f32[72,128]{1,0:T(8,...) custom-call(f32[96,128]{1,0:T(8,128)S(1)} %copy-done, f32[96,128]{1,0:T(8,128)S(1)} %copy-done.1, ...), custom_call_target="tpu_custom_call" | custom-call | flops 4000000 | bytes 3000000 | tf_op jit(solution)/shard_map/join_rows/pallas_call | solution.py:341
  14.6 2.0 %collective-permute-start.2 = (f32[72,128]{1,0:T(8,128)S(1)}, f32[72,128]{1,0:T(8,128)S(1)}, u32[]{:S(2)}, u32[]{:S(2)}) collective-permute-start(f32[72,128]{1,0:T(8,128)S(1)} %get-tuple-element.35), channel_id=1, source_target_pairs={{0,31},{1,2},{2,1},{3,4},{4,3},{5,6},{6,5},{7,8},{8,7},{9,10},{10,... | collective-permute-start | bytes 110600 | tf_op jit(solution)/shard_map/ppermute | solution.py:347
  16.6 0.1 collective-permute-start.3
  16.7 0.8 %second_step.1.u2 = f32[2,16,64,128]{3,2,1,0:T(8,128)S(1)} custom-call(f32[16,64,128]{2,1,0:T(8,128)S(1)} %get-tuple-element.23.u1_0, f32[16,64,128]{2,1,0:T(8,128)S(1)} %get-tuple-element.24.u1_1, s32[16,64,128]{2,1,0:T(8,128)S(1)} %get-tuple-element.25.mask, f32[16,64,128]{2,1,0:T(8,128)S(1)} %get-tuple-element.26.east, ...), custom_call_target="tpu_custom_call" | custom-call | flops 8000000 | bytes 6000000 | tf_op jit(solution)/shard_map/second_step/pallas_call | solution.py:350
  17.5 2.6 %collective-permute-done.2.got_2 = f32[72,128]{1,0:T(8,128)S(1)} collective-permute-done((f32[72,128]{1,0:T(8,128)S(1)}, f32[72,128]{1,0:T(8,128)S(1)}, u32[]{:S(2)}, u32[]{:S(2)}) %collective-permute-start.2) | collective-permute-done | bytes 36896 | tf_op jit(solution)/shard_map/ppermute | solution.py:347
  20.1 0.0 collective-permute-done.3.got_1
  20.1 1.3 %join_columns.1 = f32[2,16,64,128]{3,2,1,0:T(8,128)} custom-call(f32[2,16,64,128]{3,2,1,0:T(8,128)S(1)} %second_step.1.u2, f32[72,128]{1,0:T(8,128)S(1)} %collective-permute-done.2.got_2, f32[72,128]{1,0:T(8,128)S(1)} %collective-permute-done.3.got_1, f32[72,128]{1,0:T(8,128)S(1)} %get-tuple-element.37.values, f32[72,128]{1,0:T(8,128)S(1)} %get-tuple-element.38.easts, ...), custom_call_target="tpu_custom_call" | custom-call | flops 4000000 | bytes 3000000 | tf_op jit(solution)/shard_map/join_columns/pallas_call | solution.py:352
Async XLA Ops:
  1.7 11.2 %collective-permute-start = (f32[96,128]{1,0:T(8,128)}, f32[96,128]{1,0:T(8,128)S(1)}, u32[]{:S(2)}, u32[]{:S(2)}) collective-permute-start(f32[96,128]{1,0:T(8,128)} %get-tuple-element.28.own_a), channel_id=1, source_target_pairs={{32,64},{64,32},{96,128},{128,96},{160,192},{192,160},{224,255},{3... | collective-permute-start | bytes 147464 | tf_op jit(solution)/shard_map/ppermute | solution.py:330
  9.7 4.6 %copy-start = (f32[96,128]{1,0:T(8,128)S(1)}, f32[96,128]{1,0:T(8,128)}, u32[]{:S(2)}) copy-start(f32[96,128]{1,0:T(8,128)} %get-tuple-element.28.own_a) | copy-start | bytes 147460
  9.7 4.6 %copy-start.1 = (f32[96,128]{1,0:T(8,128)S(1)}, f32[96,128]{1,0:T(8,128)}, u32[]{:S(2)}) copy-start(f32[96,128]{1,0:T(8,128)} %get-tuple-element.29.own_b) | copy-start | bytes 147460
  9.7 4.6 %collective-permute-start.1 = (f32[96,128]{1,0:T(8,128)}, f32[96,128]{1,0:T(8,128)S(1)}, u32[]{:S(2)}, u32[]{:S(2)}) collective-permute-start(f32[96,128]{1,0:T(8,128)} %get-tuple-element.29.own_b), channel_id=1, source_target_pairs={{0,32},{32,0},{64,96},{96,64},{128,160},{160,128},{192,224},{224,1... | collective-permute-start | bytes 147464 | tf_op jit(solution)/shard_map/ppermute | solution.py:331
  14.6 5.6 %collective-permute-start.2 = (f32[72,128]{1,0:T(8,128)S(1)}, f32[72,128]{1,0:T(8,128)S(1)}, u32[]{:S(2)}, u32[]{:S(2)}) collective-permute-start(f32[72,128]{1,0:T(8,128)S(1)} %get-tuple-element.35), channel_id=1, source_target_pairs={{0,31},{1,2},{2,1},{3,4},{4,3},{5,6},{6,5},{7,8},{8,7},{9,10},{10,... | collective-permute-start | bytes 110600 | tf_op jit(solution)/shard_map/ppermute | solution.py:347
  16.6 3.5 %collective-permute-start.3 = (f32[72,128]{1,0:T(8,128)S(1)}, f32[72,128]{1,0:T(8,128)S(1)}, u32[]{:S(2)}, u32[]{:S(2)}) collective-permute-start(f32[72,128]{1,0:T(8,128)S(1)} %get-tuple-element.36), channel_id=1, source_target_pairs={{0,1},{1,0},{2,3},{3,2},{4,5},{5,4},{6,7},{7,6},{8,9},{9,8},{10,11... | collective-permute-start | bytes 110600 | tf_op jit(solution)/shard_map/ppermute | solution.py:348

commit v4 on v3

--- a/solution.py
+++ b/solution.py
@@ -79,7 +79,7 @@
 
 
 CHUNK = 4
-FETCH = 4
+FETCH = 8
 
 
 def first_step(
@@ -87,16 +87,18 @@
 ):
     out_u = (out_u0, out_u1)
 
-    def copies(c):
+    def copies(c, which):
         span = pl.ds(c * FETCH, FETCH)
         pairs = [(noise.at[0, span], out_u0.at[span]), (noise.at[1, span], out_u1.at[span])]
         pairs += [(mask.at[span], held_mask.at[span]), (east.at[span], held_east.at[span])]
         pairs += [(north.at[span], held_north.at[span])]
-        return [pltpu.make_async_copy(a, b, sem.at[c, k]) for k, (a, b) in enumerate(pairs)]
-
-    for c in range(min(LEVELS // FETCH, 99)):
-        for copy in copies(c):
-            copy.start()
+        return [pltpu.make_async_copy(*pairs[k], sem.at[c, k]) for k in which]
+
+    fields, coefs = range(2), range(2, 5)
+    for which in (coefs, fields):
+        for c in range(LEVELS // FETCH):
+            for copy in copies(c, which):
+                copy.start()
     lane = lanes(ROWS)
     row = lax.broadcasted_iota(jnp.int32, (ROWS, COLS), 0)
     group = lane // 4
@@ -122,17 +124,20 @@
             edges[m * LEVELS + l] = jnp.where(lane == COLS - 2, u_e, jnp.where(lane == 1, u_w, v))
 
     for c in range(LEVELS // FETCH):
-        for copy in copies(c):
+        for copy in copies(c, coefs):
+            copy.wait()
+        for l in range(c * FETCH, (c + 1) * FETCH):
+            k = held_mask[l].astype(F32)
+            place(out_east, held_east[l] * k, l)
+            place(out_north, held_north[l], l)
+            place(out_mask, k, l)
+    for c in range(LEVELS // FETCH):
+        for copy in copies(c, fields):
             copy.wait()
         for l in range(c * FETCH, (c + 1) * FETCH):
             level(l)
-    for l in range(LEVELS):
-        k = held_mask[l].astype(F32)
-        place(out_east, held_east[l] * k, l)
-        place(out_north, held_north[l], l)
-        place(out_mask, k, l)
-        for m in range(2):
-            place(out_values, edges[m * LEVELS + l], m * LEVELS + l)
+    for g in range(2 * LEVELS):
+        place(out_values, edges[g], g)
     for out in (out_east, out_north, out_mask):
         out[...] = jnp.where(lane < 64, out[...], turned(out[...], 64))
 
@@ -300,7 +305,7 @@
         out_specs=[VMEM if body is not join_columns else HBM] * len(outputs),
         out_shape=outputs,
         scratch_shapes=list(scratch),
-        compiler_params=pltpu.CompilerParams(vmem_limit_bytes=limit * 1024 * 1024),
+        compiler_params=pltpu.CompilerParams(vmem_limit_bytes=int(limit * 1024 * 1024)),
         cost_estimate=pl.CostEstimate(flops=int(us * 4e6), bytes_accessed=int(us * 3e6), transcendentals=0),
         name=name,
     )
@@ -317,7 +322,7 @@
         ends,
         pltpu.SemaphoreType.DMA((4, 2)),
     ]
-    send_a, send_b = kernel(edge_rows, "edge_rows", 4, [message] * 2, 1, scratch, HBM, 63)(
+    send_a, send_b = kernel(edge_rows, "edge_rows", 4, [message] * 2, 1, scratch, HBM, 53.5)(
         noise, land_mask, east_coef, north_coef
     )
 

time: 21.7 us -> 20.8 us (0.959)
  Pallas kernels: 7.32 us -> 6.49 us
    pallas_call x1, Pallas kernels: 1.72 us -> 1.1 us  [local(): kernel(edge_rows, 'edge_rows', 4, [message] * 2, 1, scratch, HBM, 53.5)]
  transfers between devices with their start and end apart: 4 -> 4, of which waited for: 2 -> 2; matrix products, arithmetic and copies ran while one was open for 0% -> 0% of each run, Pallas kernels for 19% -> 18%
where the time goes in v4:
time: 20.8 us; the launch traced here: 20.6 us
  starting transfers between devices  10.1 us (49%)
  Pallas kernels  6.49 us (31%)
  waiting for transfers between devices  3.97 us (19%)
    ppermute x1, starting transfers between devices, local(): got_a = lax.ppermute(send_a, ('lat', 'lon'), route_a)  7.92 us
    pallas_call x1, Pallas kernels, local(): kernel(first_step, 'first_step', 4, outs, 2, scratch, HBM, 51)  2.96 us
    ppermute x1, waiting for transfers between devices, local(): got_2 = lax.ppermute(send_2, 'lon', route_2)  2.63 us
    ppermute x1, starting transfers between devices, local(): got_2 = lax.ppermute(send_2, 'lon', route_2)  2.05 us
    pallas_call x1, Pallas kernels, local(): kernel(join_columns, 'join_columns', 7, [whole], 1, scratch)  1.34 us
    ppermute x1, waiting for transfers between devices, local(): got_b = lax.ppermute(send_b, 'lat', route_b)  1.33 us
    pallas_call x1, Pallas kernels, local(): kernel(edge_rows, 'edge_rows', 4, [message] * 2, 1, scratch, HBM, 53.5)  1.1 us
    pallas_call x1, Pallas kernels, local(): kernel(second_step, 'second_step', 6, [whole], 2)  0.83 us
  transfers between devices with their start and end apart: 4, of which 2 were waited for; matrix products, arithmetic and copies ran while one was open for 0% of the time, Pallas kernels for 18%

profile of v4, /device:TPU:22, one launch (start us, length us, event | category | flops | bytes accessed | tf_op | source)
XLA Modules:
  0.0 20.6 jit_solution(2568116649114593220)
XLA Ops:
  0.0 1.1 %edge_rows.1 = (f32[96,128]{1,0:T(8,128)S(1)}, f32[96,128]{1,0:T(8,128)S(1)}) custom-call(f32[2,16,64,128]{3,2,1,0:T(8,128)} %noise.3, s32[16,64,128]{2,1,0:T(8,128)} %mask.3, f32[16,64,128]{2,1,0:T(8,128)} %east.3, f32[16,64,128]{2,1,0:T(8,128)} %north.3), custom_call_target="tpu_custom_call" | custom-call | flops 4000000 | bytes 3000000 | tf_op jit(solution)/shard_map/edge_rows/pallas_call | solution.py:325
  1.1 7.9 %collective-permute-start = (f32[96,128]{1,0:T(8,128)S(1)}, f32[96,128]{1,0:T(8,128)S(1)}, u32[]{:S(2)}, u32[]{:S(2)}) collective-permute-start(f32[96,128]{1,0:T(8,128)S(1)} %get-tuple-element.28.own_a), channel_id=1, source_target_pairs={{32,64},{64,32},{96,128},{128,96},{160,192},{192,160},{224,255},{3... | collective-permute-start | bytes 147464 | tf_op jit(solution)/shard_map/ppermute | solution.py:335
  9.0 0.1 collective-permute-start.1
  9.1 3.0 %first_step.1 = (f32[16,64,128]{2,1,0:T(8,128)S(1)}, f32[16,64,128]{2,1,0:T(8,128)S(1)}, f32[64,128]{1,0:T(8,128)S(1)}, f32[64,128]{1,0:T(8,128)S(1)}, f32[64,12...) custom-call(f32[2,16,64,128]{3,2,1,0:T(8,128)} %noise.3, ...), custom_call_target="tpu_custom_call" | custom-call | flops 8000000 | bytes 6000000 | tf_op jit(solution)/shard_map/first_step/pallas_call | solution.py:342
  12.1 0.0 collective-permute-done.got_a
  12.1 1.3 %collective-permute-done.1.got_b = f32[96,128]{1,0:T(8,128)S(1)} collective-permute-done((f32[96,128]{1,0:T(8,128)S(1)}, f32[96,128]{1,0:T(8,128)S(1)}, u32[]{:S(2)}, u32[]{:S(2)}) %collective-permute-start.1) | collective-permute-done | bytes 49184 | tf_op jit(solution)/shard_map/ppermute | solution.py:336
  13.4 0.3 %join_rows.1 = (f32[72,128]{1,0:T(8,128)S(1)}, f32[72,128]{1,0:T(8,128)S(1)}, f32[72,128]{1,0:T(8,128)S(1)}, f32[72,128]{1,0:T(8,128)S(1)}, f32[72,128]{1,0:T(8,...) custom-call(f32[96,128]{1,0:T(8,128)S(1)} %get-tuple-element.28.own_a, f32[96,128]{1,0:T(8,128)S(1)} %get-tuple-element.29.own_b, ...), custom_call_target="tpu_custom_call" | custom-call | flops 4000000 | bytes 3000000 | tf_op jit(solution)/shard_map/join_rows/pallas_call | solution.py:346
  13.7 2.0 %collective-permute-start.2 = (f32[72,128]{1,0:T(8,128)S(1)}, f32[72,128]{1,0:T(8,128)S(1)}, u32[]{:S(2)}, u32[]{:S(2)}) collective-permute-start(f32[72,128]{1,0:T(8,128)S(1)} %get-tuple-element.35), channel_id=1, source_target_pairs={{0,31},{1,2},{2,1},{3,4},{4,3},{5,6},{6,5},{7,8},{8,7},{9,10},{10,... | collective-permute-start | bytes 110600 | tf_op jit(solution)/shard_map/ppermute | solution.py:352
  15.8 0.0 collective-permute-start.3
  15.8 0.8 %second_step.1.u2 = f32[2,16,64,128]{3,2,1,0:T(8,128)S(1)} custom-call(f32[16,64,128]{2,1,0:T(8,128)S(1)} %get-tuple-element.23.u1_0, f32[16,64,128]{2,1,0:T(8,128)S(1)} %get-tuple-element.24.u1_1, s32[16,64,128]{2,1,0:T(8,128)S(1)} %get-tuple-element.25.mask, f32[16,64,128]{2,1,0:T(8,128)S(1)} %get-tuple-element.26.east, ...), custom_call_target="tpu_custom_call" | custom-call | flops 8000000 | bytes 6000000 | tf_op jit(solution)/shard_map/second_step/pallas_call | solution.py:355
  16.6 2.6 %collective-permute-done.2.got_2 = f32[72,128]{1,0:T(8,128)S(1)} collective-permute-done((f32[72,128]{1,0:T(8,128)S(1)}, f32[72,128]{1,0:T(8,128)S(1)}, u32[]{:S(2)}, u32[]{:S(2)}) %collective-permute-start.2) | collective-permute-done | bytes 36896 | tf_op jit(solution)/shard_map/ppermute | solution.py:352
  19.3 0.0 collective-permute-done.3.got_1
  19.3 1.3 %join_columns.1 = f32[2,16,64,128]{3,2,1,0:T(8,128)} custom-call(f32[2,16,64,128]{3,2,1,0:T(8,128)S(1)} %second_step.1.u2, f32[72,128]{1,0:T(8,128)S(1)} %collective-permute-done.2.got_2, f32[72,128]{1,0:T(8,128)S(1)} %collective-permute-done.3.got_1, f32[72,128]{1,0:T(8,128)S(1)} %get-tuple-element.37.values, f32[72,128]{1,0:T(8,128)S(1)} %get-tuple-element.38.easts, ...), custom_call_target="tpu_custom_call" | custom-call | flops 4000000 | bytes 3000000 | tf_op jit(solution)/shard_map/join_columns/pallas_call | solution.py:357
Async XLA Ops:
  1.1 11.0 %collective-permute-start = (f32[96,128]{1,0:T(8,128)S(1)}, f32[96,128]{1,0:T(8,128)S(1)}, u32[]{:S(2)}, u32[]{:S(2)}) collective-permute-start(f32[96,128]{1,0:T(8,128)S(1)} %get-tuple-element.28.own_a), channel_id=1, source_target_pairs={{32,64},{64,32},{96,128},{128,96},{160,192},{192,160},{224,255},{3... | collective-permute-start | bytes 147464 | tf_op jit(solution)/shard_map/ppermute | solution.py:335
  9.0 4.4 %collective-permute-start.1 = (f32[96,128]{1,0:T(8,128)S(1)}, f32[96,128]{1,0:T(8,128)S(1)}, u32[]{:S(2)}, u32[]{:S(2)}) collective-permute-start(f32[96,128]{1,0:T(8,128)S(1)} %get-tuple-element.29.own_b), channel_id=1, source_target_pairs={{0,32},{32,0},{64,96},{96,64},{128,160},{160,128},{192,224},{224,1... | collective-permute-start | bytes 147464 | tf_op jit(solution)/shard_map/ppermute | solution.py:336
  13.7 5.6 %collective-permute-start.2 = (f32[72,128]{1,0:T(8,128)S(1)}, f32[72,128]{1,0:T(8,128)S(1)}, u32[]{:S(2)}, u32[]{:S(2)}) collective-permute-start(f32[72,128]{1,0:T(8,128)S(1)} %get-tuple-element.35), channel_id=1, source_target_pairs={{0,31},{1,2},{2,1},{3,4},{4,3},{5,6},{6,5},{7,8},{8,7},{9,10},{10,... | collective-permute-start | bytes 110600 | tf_op jit(solution)/shard_map/ppermute | solution.py:352
  15.8 3.5 %collective-permute-start.3 = (f32[72,128]{1,0:T(8,128)S(1)}, f32[72,128]{1,0:T(8,128)S(1)}, u32[]{:S(2)}, u32[]{:S(2)}) collective-permute-start(f32[72,128]{1,0:T(8,128)S(1)} %get-tuple-element.36), channel_id=1, source_target_pairs={{0,1},{1,0},{2,3},{3,2},{4,5},{5,4},{6,7},{7,6},{8,9},{9,8},{10,11... | collective-permute-start | bytes 110600 | tf_op jit(solution)/shard_map/ppermute | solution.py:353

commit v5 on v4

--- a/solution.py
+++ b/solution.py
@@ -26,7 +26,7 @@
     return pltpu.roll(x, shift % x.shape[0], 0)
 
 
-def edge_rows(noise, mask, east, north, out_a, out_b, noise_at, mask_at, east_at, north_at, sem):
+def edge_rows(noise, mask, east, north, out_b, out_a, noise_at, mask_at, east_at, north_at, sem):
     copies = []
     for k, (whole, part) in enumerate(((noise, noise_at), (mask, mask_at), (east, east_at), (north, north_at))):
         for end in range(2):
@@ -143,7 +143,7 @@
 
 
 def join_rows(
-    own_a, own_b, got_a, got_b, values, easts, norths, masks,
+    own_b, own_a, got_b, got_a, values, easts, norths, masks,
     send_2, send_1, out_values, out_east, out_north, out_mask, out_rows, south, north, side
 ):
     lat = lax.axis_index("lat")
@@ -322,7 +322,7 @@
         ends,
         pltpu.SemaphoreType.DMA((4, 2)),
     ]
-    send_a, send_b = kernel(edge_rows, "edge_rows", 4, [message] * 2, 1, scratch, HBM, 53.5)(
+    send_b, send_a = kernel(edge_rows, "edge_rows", 4, [message] * 2, 1, scratch, HBM, 53.5)(
         noise, land_mask, east_coef, north_coef
     )
 
@@ -345,7 +345,7 @@
     square = pltpu.VMEM((COLS, COLS), F32)
     send_2, send_1, *columns, rows = kernel(
         join_rows, "join_rows", 8, [packed] * 6 + [struct(9 * LEVELS, COLS)], 1, [square] * 3
-    )(send_a, send_b, got_a, got_b, *columns)
+    )(send_b, send_a, got_b, got_a, *columns)
 
     route_1 = [(k, k ^ 1) for k in range(n_lon)]
     route_2 = [(k, (((k + n_lon - 1) % n_lon ^ 1) + 1) % n_lon) for k in range(n_lon)]

time: 20.8 us -> 20.4 us (0.981)
  the two profiles are of different devices: /device:TPU:22 before, /device:TPU:16 now
where the time goes in v5:
time: 20.4 us; the launch traced here: 20.2 us
  starting transfers between devices  9.99 us (49%)
  Pallas kernels  6.49 us (32%)
  waiting for transfers between devices  3.64 us (18%)
    ppermute x1, starting transfers between devices, local(): got_2 = lax.ppermute(send_2, 'lon', route_2)  4.64 us
    ppermute x1, starting transfers between devices, local(): got_a = lax.ppermute(send_a, ('lat', 'lon'), route_a)  3.76 us
    pallas_call x1, Pallas kernels, local(): kernel(first_step, 'first_step', 4, outs, 2, scratch, HBM, 51)  2.96 us
    ppermute x1, waiting for transfers between devices, local(): got_a = lax.ppermute(send_a, ('lat', 'lon'), route_a)  2.84 us
    ppermute x1, starting transfers between devices, local(): got_b = lax.ppermute(send_b, 'lat', route_b)  1.58 us
    pallas_call x1, Pallas kernels, local(): kernel(join_columns, 'join_columns', 7, [whole], 1, scratch)  1.34 us
    pallas_call x1, Pallas kernels, local(): kernel(edge_rows, 'edge_rows', 4, [message] * 2, 1, scratch, HBM, 53.5)  1.1 us
    pallas_call x1, Pallas kernels, local(): kernel(second_step, 'second_step', 6, [whole], 2)  0.83 us
  transfers between devices with their start and end apart: 4, of which 2 were waited for; matrix products, arithmetic and copies ran while one was open for 0% of the time, Pallas kernels for 19%

profile of v5, /device:TPU:16, one launch (start us, length us, event | category | flops | bytes accessed | tf_op | source)
XLA Modules:
  0.0 20.2 jit_solution(9559129692314875811)
XLA Ops:
  0.0 1.1 %edge_rows.1 = (f32[96,128]{1,0:T(8,128)S(1)}, f32[96,128]{1,0:T(8,128)S(1)}) custom-call(f32[2,16,64,128]{3,2,1,0:T(8,128)} %noise.3, s32[16,64,128]{2,1,0:T(8,128)} %mask.3, f32[16,64,128]{2,1,0:T(8,128)} %east.3, f32[16,64,128]{2,1,0:T(8,128)} %north.3), custom_call_target="tpu_custom_call" | custom-call | flops 4000000 | bytes 3000000 | tf_op jit(solution)/shard_map/edge_rows/pallas_call | solution.py:325
  1.1 1.6 %collective-permute-start = (f32[96,128]{1,0:T(8,128)S(1)}, f32[96,128]{1,0:T(8,128)S(1)}, u32[]{:S(2)}, u32[]{:S(2)}) collective-permute-start(f32[96,128]{1,0:T(8,128)S(1)} %get-tuple-element.28.own_b), channel_id=1, source_target_pairs={{0,32},{32,0},{64,96},{96,64},{128,160},{160,128},{192,224},{224,1... | collective-permute-start | bytes 147464 | tf_op jit(solution)/shard_map/ppermute | solution.py:336
  2.7 3.8 %collective-permute-start.1 = (f32[96,128]{1,0:T(8,128)S(1)}, f32[96,128]{1,0:T(8,128)S(1)}, u32[]{:S(2)}, u32[]{:S(2)}) collective-permute-start(f32[96,128]{1,0:T(8,128)S(1)} %get-tuple-element.29.own_a), channel_id=1, source_target_pairs={{32,64},{64,32},{96,128},{128,96},{160,192},{192,160},{224,255},{3... | collective-permute-start | bytes 147464 | tf_op jit(solution)/shard_map/ppermute | solution.py:335
  6.5 3.0 %first_step.1 = (f32[16,64,128]{2,1,0:T(8,128)S(1)}, f32[16,64,128]{2,1,0:T(8,128)S(1)}, f32[64,128]{1,0:T(8,128)S(1)}, f32[64,128]{1,0:T(8,128)S(1)}, f32[64,12...) custom-call(f32[2,16,64,128]{3,2,1,0:T(8,128)} %noise.3, ...), custom_call_target="tpu_custom_call" | custom-call | flops 8000000 | bytes 6000000 | tf_op jit(solution)/shard_map/first_step/pallas_call | solution.py:342
  9.4 0.0 collective-permute-done.got_b
  9.4 2.8 %collective-permute-done.1.got_a = f32[96,128]{1,0:T(8,128)S(1)} collective-permute-done((f32[96,128]{1,0:T(8,128)S(1)}, f32[96,128]{1,0:T(8,128)S(1)}, u32[]{:S(2)}, u32[]{:S(2)}) %collective-permute-start.1) | collective-permute-done | bytes 49184 | tf_op jit(solution)/shard_map/ppermute | solution.py:335
  12.3 0.3 %join_rows.1 = (f32[72,128]{1,0:T(8,128)S(1)}, f32[72,128]{1,0:T(8,128)S(1)}, f32[72,128]{1,0:T(8,128)S(1)}, f32[72,128]{1,0:T(8,128)S(1)}, f32[72,128]{1,0:T(8,...) custom-call(f32[96,128]{1,0:T(8,128)S(1)} %get-tuple-element.28.own_b, f32[96,128]{1,0:T(8,128)S(1)} %get-tuple-element.29.own_a, ...), custom_call_target="tpu_custom_call" | custom-call | flops 4000000 | bytes 3000000 | tf_op jit(solution)/shard_map/join_rows/pallas_call | solution.py:346
  12.5 4.6 %collective-permute-start.2 = (f32[72,128]{1,0:T(8,128)S(1)}, f32[72,128]{1,0:T(8,128)S(1)}, u32[]{:S(2)}, u32[]{:S(2)}) collective-permute-start(f32[72,128]{1,0:T(8,128)S(1)} %get-tuple-element.35), channel_id=1, source_target_pairs={{0,31},{1,2},{2,1},{3,4},{4,3},{5,6},{6,5},{7,8},{8,7},{9,10},{10,... | collective-permute-start | bytes 110600 | tf_op jit(solution)/shard_map/ppermute | solution.py:352
  17.2 0.0 collective-permute-start.3
  17.2 0.8 %second_step.1.u2 = f32[2,16,64,128]{3,2,1,0:T(8,128)S(1)} custom-call(f32[16,64,128]{2,1,0:T(8,128)S(1)} %get-tuple-element.23.u1_0, f32[16,64,128]{2,1,0:T(8,128)S(1)} %get-tuple-element.24.u1_1, s32[16,64,128]{2,1,0:T(8,128)S(1)} %get-tuple-element.25.mask, f32[16,64,128]{2,1,0:T(8,128)S(1)} %get-tuple-element.26.east, ...), custom_call_target="tpu_custom_call" | custom-call | flops 8000000 | bytes 6000000 | tf_op jit(solution)/shard_map/second_step/pallas_call | solution.py:355
  18.0 0.8 %collective-permute-done.2.got_2 = f32[72,128]{1,0:T(8,128)S(1)} collective-permute-done((f32[72,128]{1,0:T(8,128)S(1)}, f32[72,128]{1,0:T(8,128)S(1)}, u32[]{:S(2)}, u32[]{:S(2)}) %collective-permute-start.2) | collective-permute-done | bytes 36896 | tf_op jit(solution)/shard_map/ppermute | solution.py:352
  18.8 0.0 collective-permute-done.3.got_1
  18.8 1.3 %join_columns.1 = f32[2,16,64,128]{3,2,1,0:T(8,128)} custom-call(f32[2,16,64,128]{3,2,1,0:T(8,128)S(1)} %second_step.1.u2, f32[72,128]{1,0:T(8,128)S(1)} %collective-permute-done.2.got_2, f32[72,128]{1,0:T(8,128)S(1)} %collective-permute-done.3.got_1, f32[72,128]{1,0:T(8,128)S(1)} %get-tuple-element.37.values, f32[72,128]{1,0:T(8,128)S(1)} %get-tuple-element.38.easts, ...), custom_call_target="tpu_custom_call" | custom-call | flops 4000000 | bytes 3000000 | tf_op jit(solution)/shard_map/join_columns/pallas_call | solution.py:357
Async XLA Ops:
  1.1 8.3 %collective-permute-start = (f32[96,128]{1,0:T(8,128)S(1)}, f32[96,128]{1,0:T(8,128)S(1)}, u32[]{:S(2)}, u32[]{:S(2)}) collective-permute-start(f32[96,128]{1,0:T(8,128)S(1)} %get-tuple-element.28.own_b), channel_id=1, source_target_pairs={{0,32},{32,0},{64,96},{96,64},{128,160},{160,128},{192,224},{224,1... | collective-permute-start | bytes 147464 | tf_op jit(solution)/shard_map/ppermute | solution.py:336
  2.7 9.6 %collective-permute-start.1 = (f32[96,128]{1,0:T(8,128)S(1)}, f32[96,128]{1,0:T(8,128)S(1)}, u32[]{:S(2)}, u32[]{:S(2)}) collective-permute-start(f32[96,128]{1,0:T(8,128)S(1)} %get-tuple-element.29.own_a), channel_id=1, source_target_pairs={{32,64},{64,32},{96,128},{128,96},{160,192},{192,160},{224,255},{3... | collective-permute-start | bytes 147464 | tf_op jit(solution)/shard_map/ppermute | solution.py:335
  12.5 6.3 %collective-permute-start.2 = (f32[72,128]{1,0:T(8,128)S(1)}, f32[72,128]{1,0:T(8,128)S(1)}, u32[]{:S(2)}, u32[]{:S(2)}) collective-permute-start(f32[72,128]{1,0:T(8,128)S(1)} %get-tuple-element.35), channel_id=1, source_target_pairs={{0,31},{1,2},{2,1},{3,4},{4,3},{5,6},{6,5},{7,8},{8,7},{9,10},{10,... | collective-permute-start | bytes 110600 | tf_op jit(solution)/shard_map/ppermute | solution.py:352
  17.2 1.6 %collective-permute-start.3 = (f32[72,128]{1,0:T(8,128)S(1)}, f32[72,128]{1,0:T(8,128)S(1)}, u32[]{:S(2)}, u32[]{:S(2)}) collective-permute-start(f32[72,128]{1,0:T(8,128)S(1)} %get-tuple-element.36), channel_id=1, source_target_pairs={{0,1},{1,0},{2,3},{3,2},{4,5},{5,4},{6,7},{7,6},{8,9},{9,8},{10,11... | collective-permute-start | bytes 110600 | tf_op jit(solution)/shard_map/ppermute | solution.py:353

commit v6 on v5

--- a/solution.py
+++ b/solution.py
@@ -68,10 +68,18 @@
         v = noise_at[0, m, :, 1, :] * mask_b2
         bottom.append(u)
         bottom_p.append(mask_b * (u + lateral(u, east_b, west_b) + north_b * (v - u)))
-    top += top_p + [north_at[1, :, 1, :] * mask_t, full_t * mask_t]
-    bottom += bottom_p + [mask_b, full_b * mask_b]
+    top += top_p + [north_at[1, :, 1, :] * mask_t]
+    bottom += bottom_p + [mask_b]
     flip = jnp.where(top_block, COLS - 1 - lane, lane)
-    for q in range(6):
+    def last_column(x):
+        level = lax.broadcasted_iota(jnp.int32, (LEVELS, COLS), 0)
+        return jnp.sum(jnp.where(lane == level, x[:, COLS - 1 :], 0.0), axis=0, keepdims=True)
+
+    face_t, face_b = last_column(full_t * mask_t), last_column(full_b * mask_b)
+    tail = pl.ds(5 * LEVELS, 8)
+    out_b[tail, :] = jnp.broadcast_to(jnp.where(even, face_t, face_b), (8, COLS))
+    out_a[tail, :] = jnp.broadcast_to(jnp.where(even, face_b, face_t), (8, COLS))
+    for q in range(5):
         rows = pl.ds(q * LEVELS, LEVELS)
         out_b[rows, :] = jnp.where(even, top[q], bottom[q])
         crossed = jnp.take_along_axis(top[q], flip, axis=1)
@@ -185,10 +193,11 @@
         put(north, m, (0, 3), up)
         put(north, m, (1, 2), gain_n)
     out_rows[pl.ds(8 * LEVELS, LEVELS), :] = far_s
-    _, _, up_e, down_e = part(5)
-    put(side, 0, (0, 1), down_e)
     put(side, 0, (2, 3), far_s)
-    put(side, 1, (0, 1, 2, 3), up_e)
+    tail = pl.ds(5 * LEVELS, 8)
+    spread = lax.rem(lanes(8), 64) // 4
+    up_e = jnp.take_along_axis(jnp.where(even, got_b[tail, :], got_a[tail, :]), spread, axis=1)
+    down_e = jnp.take_along_axis(jnp.where(even, got_a[tail, :], got_b[tail, :]), spread, axis=1)
 
     lane1 = lanes(1)
     slot1 = lax.rem(lane1, 4)
@@ -200,11 +209,9 @@
     inner = (slot1 == 1) | (slot1 == 2)
     low_half = lane1 < 64
     first_c, last_c = turned_c[0:1, :], turned_c[COLS - 1 : COLS, :]
-    face_s = jnp.where(low_half, last_c, turned(last_c, 64))
+    face_s, face_n = down_e[0:1, :], up_e[0:1, :]
     coef_s = jnp.where(slot1 == 1, turned(last_c, -1), first_c)
     coef_s = jnp.where(low_half, coef_s, turned(coef_s, 64))
-    face_n = jnp.where(low_half, turned(last_c, 64), last_c)
-    mirrored = jnp.where(low_half, turned(first_c, 64), first_c)
 
     def extend(out, x, north_row, south_row):
         out[0:ROWS, :] = x[...]
@@ -217,7 +224,7 @@
     out_values[0:1, :] = values[0:1, :] + jnp.where(inner, row_s, 0.0)
     out_values[ROWS - 1 : ROWS, :] = values[ROWS - 1 : ROWS, :] + jnp.where(inner, row_n, 0.0)
     extend(out_east, easts, jnp.where(top_block, one, face_n), face_s)
-    extend(out_mask, masks, jnp.where(top_block, mirrored, one), one)
+    extend(out_mask, masks, jnp.where(top_block, face_n, one), one)
     extend(out_north, norths, jnp.zeros((1, COLS), F32), coef_s)
     slot = lax.rem(lanes(PACKED), 4)
     x = out_values[...]
@@ -313,7 +320,7 @@
 
 def local(noise, land_mask, east_coef, north_coef):
     n_lat, n_lon = lax.axis_size("lat"), lax.axis_size("lon")
-    message = struct(6 * LEVELS, COLS)
+    message = struct(5 * LEVELS + 8, COLS)
     ends = pltpu.VMEM((2, LEVELS, 2, COLS), F32)
     scratch = [
         pltpu.VMEM((2, 2, LEVELS, 2, COLS), F32),

time: 20.4 us -> 20.3 us (level)
  no operation moved by 1% of the time
where the time goes in v6:
time: 20.3 us; the launch traced here: 20.1 us
  starting transfers between devices  9.99 us (49%)
  Pallas kernels  6.5 us (32%)
  waiting for transfers between devices  3.6 us (18%)
    ppermute x1, starting transfers between devices, local(): got_2 = lax.ppermute(send_2, 'lon', route_2)  4.64 us
    ppermute x1, starting transfers between devices, local(): got_a = lax.ppermute(send_a, ('lat', 'lon'), route_a)  3.76 us
    pallas_call x1, Pallas kernels, local(): kernel(first_step, 'first_step', 4, outs, 2, scratch, HBM, 51)  2.96 us
    ppermute x1, waiting for transfers between devices, local(): got_a = lax.ppermute(send_a, ('lat', 'lon'), route_a)  2.79 us
    ppermute x1, starting transfers between devices, local(): got_b = lax.ppermute(send_b, 'lat', route_b)  1.58 us
    pallas_call x1, Pallas kernels, local(): kernel(join_columns, 'join_columns', 7, [whole], 1, scratch)  1.34 us
    pallas_call x1, Pallas kernels, local(): kernel(edge_rows, 'edge_rows', 4, [message] * 2, 1, scratch, HBM, 53.5)  1.1 us
    pallas_call x1, Pallas kernels, local(): kernel(second_step, 'second_step', 6, [whole], 2)  0.83 us
  transfers between devices with their start and end apart: 4, of which 2 were waited for; matrix products, arithmetic and copies ran while one was open for 0% of the time, Pallas kernels for 19%

profile of v6, /device:TPU:16, one launch (start us, length us, event | category | flops | bytes accessed | tf_op | source)
XLA Modules:
  0.0 20.1 jit_solution(1757327167193330045)
XLA Ops:
  0.0 1.1 %edge_rows.1 = (f32[88,128]{1,0:T(8,128)S(1)}, f32[88,128]{1,0:T(8,128)S(1)}) custom-call(f32[2,16,64,128]{3,2,1,0:T(8,128)} %noise.3, s32[16,64,128]{2,1,0:T(8,128)} %mask.3, f32[16,64,128]{2,1,0:T(8,128)} %east.3, f32[16,64,128]{2,1,0:T(8,128)} %north.3), custom_call_target="tpu_custom_call" | custom-call | flops 4000000 | bytes 3000000 | tf_op jit(solution)/shard_map/edge_rows/pallas_call | solution.py:332
  1.1 1.6 %collective-permute-start = (f32[88,128]{1,0:T(8,128)S(1)}, f32[88,128]{1,0:T(8,128)S(1)}, u32[]{:S(2)}, u32[]{:S(2)}) collective-permute-start(f32[88,128]{1,0:T(8,128)S(1)} %get-tuple-element.28.own_b), channel_id=1, source_target_pairs={{0,32},{32,0},{64,96},{96,64},{128,160},{160,128},{192,224},{224,1... | collective-permute-start | bytes 135176 | tf_op jit(solution)/shard_map/ppermute | solution.py:343
  2.7 3.8 %collective-permute-start.1 = (f32[88,128]{1,0:T(8,128)S(1)}, f32[88,128]{1,0:T(8,128)S(1)}, u32[]{:S(2)}, u32[]{:S(2)}) collective-permute-start(f32[88,128]{1,0:T(8,128)S(1)} %get-tuple-element.29.own_a), channel_id=1, source_target_pairs={{32,64},{64,32},{96,128},{128,96},{160,192},{192,160},{224,255},{3... | collective-permute-start | bytes 135176 | tf_op jit(solution)/shard_map/ppermute | solution.py:342
  6.5 3.0 %first_step.1 = (f32[16,64,128]{2,1,0:T(8,128)S(1)}, f32[16,64,128]{2,1,0:T(8,128)S(1)}, f32[64,128]{1,0:T(8,128)S(1)}, f32[64,128]{1,0:T(8,128)S(1)}, f32[64,12...) custom-call(f32[2,16,64,128]{3,2,1,0:T(8,128)} %noise.3, ...), custom_call_target="tpu_custom_call" | custom-call | flops 8000000 | bytes 6000000 | tf_op jit(solution)/shard_map/first_step/pallas_call | solution.py:349
  9.4 0.0 collective-permute-done.got_b
  9.4 2.8 %collective-permute-done.1.got_a = f32[88,128]{1,0:T(8,128)S(1)} collective-permute-done((f32[88,128]{1,0:T(8,128)S(1)}, f32[88,128]{1,0:T(8,128)S(1)}, u32[]{:S(2)}, u32[]{:S(2)}) %collective-permute-start.1) | collective-permute-done | bytes 45088 | tf_op jit(solution)/shard_map/ppermute | solution.py:342
  12.2 0.3 %join_rows.1 = (f32[72,128]{1,0:T(8,128)S(1)}, f32[72,128]{1,0:T(8,128)S(1)}, f32[72,128]{1,0:T(8,128)S(1)}, f32[72,128]{1,0:T(8,128)S(1)}, f32[72,128]{1,0:T(8,...) custom-call(f32[88,128]{1,0:T(8,128)S(1)} %get-tuple-element.28.own_b, f32[88,128]{1,0:T(8,128)S(1)} %get-tuple-element.29.own_a, ...), custom_call_target="tpu_custom_call" | custom-call | flops 4000000 | bytes 3000000 | tf_op jit(solution)/shard_map/join_rows/pallas_call | solution.py:353
  12.5 4.6 %collective-permute-start.2 = (f32[72,128]{1,0:T(8,128)S(1)}, f32[72,128]{1,0:T(8,128)S(1)}, u32[]{:S(2)}, u32[]{:S(2)}) collective-permute-start(f32[72,128]{1,0:T(8,128)S(1)} %get-tuple-element.35), channel_id=1, source_target_pairs={{0,31},{1,2},{2,1},{3,4},{4,3},{5,6},{6,5},{7,8},{8,7},{9,10},{10,... | collective-permute-start | bytes 110600 | tf_op jit(solution)/shard_map/ppermute | solution.py:359
  17.1 0.0 collective-permute-start.3
  17.1 0.8 %second_step.1.u2 = f32[2,16,64,128]{3,2,1,0:T(8,128)S(1)} custom-call(f32[16,64,128]{2,1,0:T(8,128)S(1)} %get-tuple-element.23.u1_0, f32[16,64,128]{2,1,0:T(8,128)S(1)} %get-tuple-element.24.u1_1, s32[16,64,128]{2,1,0:T(8,128)S(1)} %get-tuple-element.25.mask, f32[16,64,128]{2,1,0:T(8,128)S(1)} %get-tuple-element.26.east, ...), custom_call_target="tpu_custom_call" | custom-call | flops 8000000 | bytes 6000000 | tf_op jit(solution)/shard_map/second_step/pallas_call | solution.py:362
  18.0 0.8 %collective-permute-done.2.got_2 = f32[72,128]{1,0:T(8,128)S(1)} collective-permute-done((f32[72,128]{1,0:T(8,128)S(1)}, f32[72,128]{1,0:T(8,128)S(1)}, u32[]{:S(2)}, u32[]{:S(2)}) %collective-permute-start.2) | collective-permute-done | bytes 36896 | tf_op jit(solution)/shard_map/ppermute | solution.py:359
  18.8 0.0 collective-permute-done.3.got_1
  18.8 1.3 %join_columns.1 = f32[2,16,64,128]{3,2,1,0:T(8,128)} custom-call(f32[2,16,64,128]{3,2,1,0:T(8,128)S(1)} %second_step.1.u2, f32[72,128]{1,0:T(8,128)S(1)} %collective-permute-done.2.got_2, f32[72,128]{1,0:T(8,128)S(1)} %collective-permute-done.3.got_1, f32[72,128]{1,0:T(8,128)S(1)} %get-tuple-element.37.values, f32[72,128]{1,0:T(8,128)S(1)} %get-tuple-element.38.easts, ...), custom_call_target="tpu_custom_call" | custom-call | flops 4000000 | bytes 3000000 | tf_op jit(solution)/shard_map/join_columns/pallas_call | solution.py:364
Async XLA Ops:
  1.1 8.3 %collective-permute-start = (f32[88,128]{1,0:T(8,128)S(1)}, f32[88,128]{1,0:T(8,128)S(1)}, u32[]{:S(2)}, u32[]{:S(2)}) collective-permute-start(f32[88,128]{1,0:T(8,128)S(1)} %get-tuple-element.28.own_b), channel_id=1, source_target_pairs={{0,32},{32,0},{64,96},{96,64},{128,160},{160,128},{192,224},{224,1... | collective-permute-start | bytes 135176 | tf_op jit(solution)/shard_map/ppermute | solution.py:343
  2.7 9.5 %collective-permute-start.1 = (f32[88,128]{1,0:T(8,128)S(1)}, f32[88,128]{1,0:T(8,128)S(1)}, u32[]{:S(2)}, u32[]{:S(2)}) collective-permute-start(f32[88,128]{1,0:T(8,128)S(1)} %get-tuple-element.29.own_a), channel_id=1, source_target_pairs={{32,64},{64,32},{96,128},{128,96},{160,192},{192,160},{224,255},{3... | collective-permute-start | bytes 135176 | tf_op jit(solution)/shard_map/ppermute | solution.py:342
  12.5 6.3 %collective-permute-start.2 = (f32[72,128]{1,0:T(8,128)S(1)}, f32[72,128]{1,0:T(8,128)S(1)}, u32[]{:S(2)}, u32[]{:S(2)}) collective-permute-start(f32[72,128]{1,0:T(8,128)S(1)} %get-tuple-element.35), channel_id=1, source_target_pairs={{0,31},{1,2},{2,1},{3,4},{4,3},{5,6},{6,5},{7,8},{8,7},{9,10},{10,... | collective-permute-start | bytes 110600 | tf_op jit(solution)/shard_map/ppermute | solution.py:359
  17.1 1.6 %collective-permute-start.3 = (f32[72,128]{1,0:T(8,128)S(1)}, f32[72,128]{1,0:T(8,128)S(1)}, u32[]{:S(2)}, u32[]{:S(2)}) collective-permute-start(f32[72,128]{1,0:T(8,128)S(1)} %get-tuple-element.36), channel_id=1, source_target_pairs={{0,1},{1,0},{2,3},{3,2},{4,5},{5,4},{6,7},{7,6},{8,9},{9,8},{10,11... | collective-permute-start | bytes 110600 | tf_op jit(solution)/shard_map/ppermute | solution.py:360

commit v7 on v6

--- a/solution.py
+++ b/solution.py
@@ -263,7 +263,7 @@
         level(l)
 
 
-def join_columns(u2, got_2, got_1, values, easts, norths, masks, out, gain, held, sem):
+def join_columns(u2, got_2, got_1, values, easts, norths, masks, out, held, sem):
     even_lon = lax.rem(lax.axis_index("lon"), 2) == 0
     slot = lax.rem(lanes(PACKED), 4)
     is_east = slot == 1
@@ -281,7 +281,7 @@
     change = d * (1.0 - inside - n - s) + face * (ghost_1 - x - d - d) + n * slid(d, -1) + s * slid(d, 1)
     beside = inside * d
     beside = jnp.where(slot == 0, turned(beside, -1), turned(beside, 1))
-    gain[...] = k * jnp.where(inner, change, beside)
+    gain = (k * jnp.where(inner, change, beside))[0:ROWS]
 
     lane = lanes(ROWS)
     edge = (lane < 2) | (lane >= COLS - 2)
@@ -293,7 +293,7 @@
     for c in range(LEVELS // CHUNK):
         for m in range(2):
             for l in range(c * CHUNK, (c + 1) * CHUNK):
-                change = turned(gain[0:ROWS, :], 126 - 64 * m - 4 * l)
+                change = turned(gain, 126 - 64 * m - 4 * l)
                 held[m, l] = u2[m, l] + jnp.where(edge, change, 0.0)
             copy(m, c).start()
     for c in range(LEVELS // CHUNK):
@@ -360,7 +360,7 @@
     got_1 = lax.ppermute(send_1, "lon", route_1)
 
     (u2,) = kernel(second_step, "second_step", 6, [whole], 2)(u1_0, u1_1, mask, east, north, rows)
-    scratch = [pltpu.VMEM((PACKED, COLS), F32), pltpu.VMEM(whole.shape, F32), pltpu.SemaphoreType.DMA((2, LEVELS // CHUNK))]
+    scratch = [pltpu.VMEM(whole.shape, F32), pltpu.SemaphoreType.DMA((2, LEVELS // CHUNK))]
     return kernel(join_columns, "join_columns", 7, [whole], 1, scratch)(u2, got_2, got_1, *columns)[0]
 
 

time: 20.3 us -> 20.3 us (level)
  no operation moved by 1% of the time
where the time goes in v7:
time: 20.3 us; the launch traced here: 20.1 us
  starting transfers between devices  9.99 us (49%)
  Pallas kernels  6.5 us (32%)
  waiting for transfers between devices  3.6 us (18%)
    ppermute x1, starting transfers between devices, local(): got_2 = lax.ppermute(send_2, 'lon', route_2)  4.64 us
    ppermute x1, starting transfers between devices, local(): got_a = lax.ppermute(send_a, ('lat', 'lon'), route_a)  3.76 us
    pallas_call x1, Pallas kernels, local(): kernel(first_step, 'first_step', 4, outs, 2, scratch, HBM, 51)  2.96 us
    ppermute x1, waiting for transfers between devices, local(): got_a = lax.ppermute(send_a, ('lat', 'lon'), route_a)  2.79 us
    ppermute x1, starting transfers between devices, local(): got_b = lax.ppermute(send_b, 'lat', route_b)  1.58 us
    pallas_call x1, Pallas kernels, local(): kernel(join_columns, 'join_columns', 7, [whole], 1, scratch)  1.34 us
    pallas_call x1, Pallas kernels, local(): kernel(edge_rows, 'edge_rows', 4, [message] * 2, 1, scratch, HBM, 53.5)  1.1 us
    pallas_call x1, Pallas kernels, local(): kernel(second_step, 'second_step', 6, [whole], 2)  0.83 us
  transfers between devices with their start and end apart: 4, of which 2 were waited for; matrix products, arithmetic and copies ran while one was open for 0% of the time, Pallas kernels for 19%

profile of v7, /device:TPU:16, one launch (start us, length us, event | category | flops | bytes accessed | tf_op | source)
XLA Modules:
  0.0 20.1 jit_solution(1757327167193330045)
XLA Ops:
  0.0 1.1 %edge_rows.1 = (f32[88,128]{1,0:T(8,128)S(1)}, f32[88,128]{1,0:T(8,128)S(1)}) custom-call(f32[2,16,64,128]{3,2,1,0:T(8,128)} %noise.3, s32[16,64,128]{2,1,0:T(8,128)} %mask.3, f32[16,64,128]{2,1,0:T(8,128)} %east.3, f32[16,64,128]{2,1,0:T(8,128)} %north.3), custom_call_target="tpu_custom_call" | custom-call | flops 4000000 | bytes 3000000 | tf_op jit(solution)/shard_map/edge_rows/pallas_call | solution.py:332
  1.1 1.6 %collective-permute-start = (f32[88,128]{1,0:T(8,128)S(1)}, f32[88,128]{1,0:T(8,128)S(1)}, u32[]{:S(2)}, u32[]{:S(2)}) collective-permute-start(f32[88,128]{1,0:T(8,128)S(1)} %get-tuple-element.28.own_b), channel_id=1, source_target_pairs={{0,32},{32,0},{64,96},{96,64},{128,160},{160,128},{192,224},{224,1... | collective-permute-start | bytes 135176 | tf_op jit(solution)/shard_map/ppermute | solution.py:343
  2.7 3.8 %collective-permute-start.1 = (f32[88,128]{1,0:T(8,128)S(1)}, f32[88,128]{1,0:T(8,128)S(1)}, u32[]{:S(2)}, u32[]{:S(2)}) collective-permute-start(f32[88,128]{1,0:T(8,128)S(1)} %get-tuple-element.29.own_a), channel_id=1, source_target_pairs={{32,64},{64,32},{96,128},{128,96},{160,192},{192,160},{224,255},{3... | collective-permute-start | bytes 135176 | tf_op jit(solution)/shard_map/ppermute | solution.py:342
  6.5 3.0 %first_step.1 = (f32[16,64,128]{2,1,0:T(8,128)S(1)}, f32[16,64,128]{2,1,0:T(8,128)S(1)}, f32[64,128]{1,0:T(8,128)S(1)}, f32[64,128]{1,0:T(8,128)S(1)}, f32[64,12...) custom-call(f32[2,16,64,128]{3,2,1,0:T(8,128)} %noise.3, ...), custom_call_target="tpu_custom_call" | custom-call | flops 8000000 | bytes 6000000 | tf_op jit(solution)/shard_map/first_step/pallas_call | solution.py:349
  9.4 0.0 collective-permute-done.got_b
  9.4 2.8 %collective-permute-done.1.got_a = f32[88,128]{1,0:T(8,128)S(1)} collective-permute-done((f32[88,128]{1,0:T(8,128)S(1)}, f32[88,128]{1,0:T(8,128)S(1)}, u32[]{:S(2)}, u32[]{:S(2)}) %collective-permute-start.1) | collective-permute-done | bytes 45088 | tf_op jit(solution)/shard_map/ppermute | solution.py:342
  12.2 0.3 %join_rows.1 = (f32[72,128]{1,0:T(8,128)S(1)}, f32[72,128]{1,0:T(8,128)S(1)}, f32[72,128]{1,0:T(8,128)S(1)}, f32[72,128]{1,0:T(8,128)S(1)}, f32[72,128]{1,0:T(8,...) custom-call(f32[88,128]{1,0:T(8,128)S(1)} %get-tuple-element.28.own_b, f32[88,128]{1,0:T(8,128)S(1)} %get-tuple-element.29.own_a, ...), custom_call_target="tpu_custom_call" | custom-call | flops 4000000 | bytes 3000000 | tf_op jit(solution)/shard_map/join_rows/pallas_call | solution.py:353
  12.5 4.6 %collective-permute-start.2 = (f32[72,128]{1,0:T(8,128)S(1)}, f32[72,128]{1,0:T(8,128)S(1)}, u32[]{:S(2)}, u32[]{:S(2)}) collective-permute-start(f32[72,128]{1,0:T(8,128)S(1)} %get-tuple-element.35), channel_id=1, source_target_pairs={{0,31},{1,2},{2,1},{3,4},{4,3},{5,6},{6,5},{7,8},{8,7},{9,10},{10,... | collective-permute-start | bytes 110600 | tf_op jit(solution)/shard_map/ppermute | solution.py:359
  17.1 0.0 collective-permute-start.3
  17.1 0.8 %second_step.1.u2 = f32[2,16,64,128]{3,2,1,0:T(8,128)S(1)} custom-call(f32[16,64,128]{2,1,0:T(8,128)S(1)} %get-tuple-element.23.u1_0, f32[16,64,128]{2,1,0:T(8,128)S(1)} %get-tuple-element.24.u1_1, s32[16,64,128]{2,1,0:T(8,128)S(1)} %get-tuple-element.25.mask, f32[16,64,128]{2,1,0:T(8,128)S(1)} %get-tuple-element.26.east, ...), custom_call_target="tpu_custom_call" | custom-call | flops 8000000 | bytes 6000000 | tf_op jit(solution)/shard_map/second_step/pallas_call | solution.py:362
  18.0 0.8 %collective-permute-done.2.got_2 = f32[72,128]{1,0:T(8,128)S(1)} collective-permute-done((f32[72,128]{1,0:T(8,128)S(1)}, f32[72,128]{1,0:T(8,128)S(1)}, u32[]{:S(2)}, u32[]{:S(2)}) %collective-permute-start.2) | collective-permute-done | bytes 36896 | tf_op jit(solution)/shard_map/ppermute | solution.py:359
  18.8 0.0 collective-permute-done.3.got_1
  18.8 1.3 %join_columns.1 = f32[2,16,64,128]{3,2,1,0:T(8,128)} custom-call(f32[2,16,64,128]{3,2,1,0:T(8,128)S(1)} %second_step.1.u2, f32[72,128]{1,0:T(8,128)S(1)} %collective-permute-done.2.got_2, f32[72,128]{1,0:T(8,128)S(1)} %collective-permute-done.3.got_1, f32[72,128]{1,0:T(8,128)S(1)} %get-tuple-element.37.values, f32[72,128]{1,0:T(8,128)S(1)} %get-tuple-element.38.easts, ...), custom_call_target="tpu_custom_call" | custom-call | flops 4000000 | bytes 3000000 | tf_op jit(solution)/shard_map/join_columns/pallas_call | solution.py:364
Async XLA Ops:
  1.1 8.3 %collective-permute-start = (f32[88,128]{1,0:T(8,128)S(1)}, f32[88,128]{1,0:T(8,128)S(1)}, u32[]{:S(2)}, u32[]{:S(2)}) collective-permute-start(f32[88,128]{1,0:T(8,128)S(1)} %get-tuple-element.28.own_b), channel_id=1, source_target_pairs={{0,32},{32,0},{64,96},{96,64},{128,160},{160,128},{192,224},{224,1... | collective-permute-start | bytes 135176 | tf_op jit(solution)/shard_map/ppermute | solution.py:343
  2.7 9.5 %collective-permute-start.1 = (f32[88,128]{1,0:T(8,128)S(1)}, f32[88,128]{1,0:T(8,128)S(1)}, u32[]{:S(2)}, u32[]{:S(2)}) collective-permute-start(f32[88,128]{1,0:T(8,128)S(1)} %get-tuple-element.29.own_a), channel_id=1, source_target_pairs={{32,64},{64,32},{96,128},{128,96},{160,192},{192,160},{224,255},{3... | collective-permute-start | bytes 135176 | tf_op jit(solution)/shard_map/ppermute | solution.py:342
  12.5 6.3 %collective-permute-start.2 = (f32[72,128]{1,0:T(8,128)S(1)}, f32[72,128]{1,0:T(8,128)S(1)}, u32[]{:S(2)}, u32[]{:S(2)}) collective-permute-start(f32[72,128]{1,0:T(8,128)S(1)} %get-tuple-element.35), channel_id=1, source_target_pairs={{0,31},{1,2},{2,1},{3,4},{4,3},{5,6},{6,5},{7,8},{8,7},{9,10},{10,... | collective-permute-start | bytes 110600 | tf_op jit(solution)/shard_map/ppermute | solution.py:359
  17.1 1.6 %collective-permute-start.3 = (f32[72,128]{1,0:T(8,128)S(1)}, f32[72,128]{1,0:T(8,128)S(1)}, u32[]{:S(2)}, u32[]{:S(2)}) collective-permute-start(f32[72,128]{1,0:T(8,128)S(1)} %get-tuple-element.36), channel_id=1, source_target_pairs={{0,1},{1,0},{2,3},{3,2},{4,5},{5,4},{6,7},{7,6},{8,9},{9,8},{10,11... | collective-permute-start | bytes 110600 | tf_op jit(solution)/shard_map/ppermute | solution.py:360
